TPU v7x, 512 devices: a whole 4x4x16 slice. The times are simulated.
512 devices in a mesh: blk: 32 (over x, y, core), head: 8 (over z_lo), rep: 2 (over z_hi).
Axes of the slice: x: 4, y: 4, z: 16 (z_hi: 2, z_lo: 8; z = z_hi * 8 + z_lo), core: 2. Of those that a mesh axis runs over, the one named last changes fastest.
Arguments:
- slab_query: bfloat16 [4096, 3072], P(('rep', 'blk', 'head')), parts along dimension 0, may hold values from -6 to 6
- slab_output: bfloat16 [4096, 3072], P(('rep', 'blk', 'head')), parts along dimension 0, may hold values from -4 to 4
- slab_cotangent: bfloat16 [4096, 3072], P(('rep', 'blk', 'head')), parts along dimension 0, may hold values from -768 to 768
- slab_logsum: float32 [4096, 24], P(('rep', 'blk'), 'head'), parts along dimension 0
- image_keys: bfloat16 [16384, 3072], P(('rep', 'blk', 'head')), parts along dimension 0, may hold values from -6 to 6
- image_values: bfloat16 [16384, 3072], P(('rep', 'blk', 'head')), parts along dimension 0, may hold values from -6 to 6
- text_query: bfloat16 [512, 3072], P('rep', 'head'), parts along dimension 0, may hold values from -6 to 6
- text_keys: bfloat16 [512, 3072], P('rep', 'head'), parts along dimension 0, may hold values from -6 to 6
- text_values: bfloat16 [512, 3072], P('rep', 'head'), parts along dimension 0, may hold values from -6 to 6
- text_output: bfloat16 [512, 3072], P('rep', 'head'), parts along dimension 0, may hold values from -4 to 4
- text_cotangent: bfloat16 [512, 3072], P('rep', 'head'), parts along dimension 0, may hold values from -768 to 768
- text_logsum: float32 [512, 24], P('rep', 'head'), parts along dimension 0
- text_count: int32 [2], P('rep'), parts along dimension 0, may hold values from 64 to 256
- slab_offsets: int32 [2], P('rep'), parts along dimension 0, may hold values from 0 to 96
Outputs:
- slab_query_grad: bfloat16 [4096, 3072], P(('rep', 'blk', 'head')), parts along dimension 0
- image_key_grad: bfloat16 [16384, 3072], P(('rep', 'blk', 'head')), parts along dimension 0
- image_value_grad: bfloat16 [16384, 3072], P(('rep', 'blk', 'head')), parts along dimension 0
- text_query_grad: bfloat16 [512, 3072], P('rep', 'head'), parts along dimension 0
- text_key_grad: bfloat16 [512, 3072], P('rep', 'head'), parts along dimension 0
- text_value_grad: bfloat16 [512, 3072], P('rep', 'head'), parts along dimension 0
There are 2 independent parts, one for each index of `rep`. A program takes and returns all parts, laid end to end along the dimension named above; each array names one. Nothing has to cross between parts.
Inputs may be any that keep to these rules, and one draw needn't show every extreme that they name: Text rows at index text_count[0] or later are padding. The slab is the 2048 consecutive image tokens from slab_offsets[0] * 64 onward.
All inputs are finite; a program needn't handle non-finite values.
Results may differ from a plain program's by a relative error of at most 0.017.
The roundings to bfloat16 on the way count: a program that leaves them out, or rounds other values in their place, can miss the bound.
Values may be sent and summed in bfloat16 or wider, within the bound.
A program may use at most 64 MiB of HBM per device.

v0:
```python
import jax
import jax.numpy as jnp
from jax import lax
from jax.sharding import PartitionSpec as P

HEAD_DIM = 128
GRID_W = 256


def from_behind(value, axis, steps):
    count = lax.axis_size(axis)
    pairs = [(source, (source + steps) % count) for source in range(count)]
    return lax.ppermute(value, axis, pairs)


def rotate(values_in, grid_row, grid_col, orient):
    row_count = values_in.shape[0]
    quarter = HEAD_DIM // 4
    halfway = HEAD_DIM // 2
    frequency = 10000.0 ** (-jnp.arange(quarter, dtype=jnp.float32) / quarter)
    angles = jnp.concatenate(
        [grid_row[:, None] * frequency[None, :], grid_col[:, None] * frequency[None, :]], axis=1
    )
    cosine = jnp.cos(angles)[:, None, :]
    sine_term = orient * jnp.sin(angles)[:, None, :]
    shaped = values_in.reshape(row_count, -1, HEAD_DIM)
    front_half = shaped[..., :halfway]
    back_half = shaped[..., halfway:]
    turned = jnp.concatenate(
        [front_half * cosine - back_half * sine_term, back_half * cosine + front_half * sine_term],
        axis=-1,
    )
    return turned.reshape(row_count, -1)


def grid_place(positions):
    return ((positions // GRID_W).astype(jnp.float32), (positions % GRID_W).astype(jnp.float32))


def row_products(cotangent, output):
    row_count = cotangent.shape[0]
    joined = cotangent.astype(jnp.float32) * output.astype(jnp.float32)
    return jnp.sum(joined.reshape(row_count, -1, HEAD_DIM), axis=-1)


def attend(queries, cotangent, logsum, deltas, key_rows, value_rows, key_mask):
    factor = HEAD_DIM ** (-0.5)
    query_count = queries.shape[0]
    key_count = key_rows.shape[0]
    head_count = logsum.shape[1]
    query_heads = queries.reshape(query_count, head_count, HEAD_DIM)
    cotan_heads = cotangent.reshape(query_count, head_count, HEAD_DIM)
    key_heads = key_rows.reshape(key_count, head_count, HEAD_DIM)
    value_heads = value_rows.reshape(key_count, head_count, HEAD_DIM)
    scores = jnp.einsum("rhd,nhd->hrn", query_heads, key_heads, preferred_element_type=jnp.float32)
    probabilities = jnp.exp(scores * factor - logsum.T[:, :, None]) * key_mask[None, None, :]
    weights = probabilities.astype(jnp.bfloat16)
    value_grad = jnp.einsum(
        "hrn,rhd->nhd", weights, cotan_heads, preferred_element_type=jnp.float32
    )
    prob_grad = jnp.einsum(
        "rhd,nhd->hrn", cotan_heads, value_heads, preferred_element_type=jnp.float32
    )
    score_grad = (probabilities * (prob_grad - deltas.T[:, :, None]) * factor).astype(jnp.bfloat16)
    query_grad = jnp.einsum(
        "hrn,nhd->rhd", score_grad, key_heads, preferred_element_type=jnp.float32
    )
    key_grad = jnp.einsum(
        "hrn,rhd->nhd", score_grad, query_heads, preferred_element_type=jnp.float32
    )
    return (
        query_grad.reshape(query_count, -1),
        key_grad.reshape(key_count, -1),
        value_grad.reshape(key_count, -1),
    )


def on_device(
    slab_query,
    slab_output,
    slab_cotangent,
    slab_logsum,
    image_keys,
    image_values,
    text_query,
    text_keys,
    text_values,
    text_output,
    text_cotangent,
    text_logsum,
    text_count,
    slab_offsets,
):
    local_query, local_output, local_cotangent, local_keys, local_values = (
        lax.all_to_all(slab_query, "head", split_axis=1, concat_axis=0, tiled=True),
        lax.all_to_all(slab_output, "head", split_axis=1, concat_axis=0, tiled=True),
        lax.all_to_all(slab_cotangent, "head", split_axis=1, concat_axis=0, tiled=True),
        lax.all_to_all(image_keys, "head", split_axis=1, concat_axis=0, tiled=True),
        lax.all_to_all(image_values, "head", split_axis=1, concat_axis=0, tiled=True),
    )
    slab_rows = local_query.shape[0]
    image_rows = local_keys.shape[0]
    text_rows = text_query.shape[0]
    loop_length = lax.axis_size("blk")
    block_place = lax.axis_index("blk")
    slab_row, slab_col = grid_place(
        (slab_offsets[0] + block_place) * slab_rows + jnp.arange(slab_rows, dtype=jnp.int32)
    )
    image_row, image_col = grid_place(
        block_place * image_rows + jnp.arange(image_rows, dtype=jnp.int32)
    )
    text_place = (GRID_W + jnp.arange(text_rows, dtype=jnp.int32)).astype(jnp.float32)
    slab_turned = rotate(local_query.astype(jnp.float32), slab_row, slab_col, 1.0).astype(
        jnp.bfloat16
    )
    image_turned = rotate(local_keys.astype(jnp.float32), image_row, image_col, 1.0).astype(
        jnp.bfloat16
    )
    text_query_turned = rotate(text_query.astype(jnp.float32), text_place, text_place, 1.0).astype(
        jnp.bfloat16
    )
    text_keys_turned = rotate(text_keys.astype(jnp.float32), text_place, text_place, 1.0).astype(
        jnp.bfloat16
    )
    slab_deltas = row_products(local_cotangent, local_output)
    text_deltas = row_products(text_cotangent, text_output)
    text_mask = (jnp.arange(text_rows, dtype=jnp.int32) < text_count[0]).astype(jnp.float32)
    image_mask = jnp.ones((image_rows,), jnp.float32)
    slab_start, text_key_part, text_value_part = attend(
        slab_turned,
        local_cotangent,
        slab_logsum,
        slab_deltas,
        text_keys_turned,
        text_values,
        text_mask,
    )
    text_query_part, image_key_acc, image_value_acc = attend(
        text_query_turned,
        text_cotangent,
        text_logsum,
        text_deltas,
        image_turned,
        local_values,
        image_mask,
    )
    text_query_sum, text_key_sum, text_value_sum = lax.psum(
        (text_query_part, text_key_part, text_value_part), "blk"
    )
    own_query, own_key, own_value = attend(
        text_query_turned,
        text_cotangent,
        text_logsum,
        text_deltas,
        text_keys_turned,
        text_values,
        text_mask,
    )
    text_query_sum = text_query_sum + own_query
    text_key_sum = text_key_sum + own_key
    text_value_sum = text_value_sum + own_value

    def hop(state):
        travel, key_acc, value_acc = state
        query_grad, key_grad, value_grad = attend(
            travel[0], travel[1], travel[2], travel[3], image_turned, local_values, image_mask
        )
        moved_query, moved_cotan = from_behind((travel[0], travel[1]), "blk", 1)
        moved_acc, moved_logsum, moved_delta = from_behind(
            (travel[4] + query_grad, travel[2], travel[3]), "blk", 1
        )
        return (
            (moved_query, moved_cotan, moved_logsum, moved_delta, moved_acc),
            key_acc + key_grad,
            value_acc + value_grad,
        )

    def two_hops(turn, state):
        return hop(hop(state))

    start_state = (
        (slab_turned, local_cotangent, slab_logsum, slab_deltas, slab_start),
        image_key_acc,
        image_value_acc,
    )
    travel, image_key_acc, image_value_acc = lax.fori_loop(
        0, loop_length // 2, two_hops, start_state
    )
    slab_acc = travel[4]
    query_back = rotate(slab_acc, slab_row, slab_col, -1.0).astype(jnp.bfloat16)
    key_back = rotate(image_key_acc, image_row, image_col, -1.0).astype(jnp.bfloat16)
    value_back = image_value_acc.astype(jnp.bfloat16)
    slab_query_grad, image_key_grad, image_value_grad = (
        lax.all_to_all(query_back, "head", split_axis=0, concat_axis=1, tiled=True),
        lax.all_to_all(key_back, "head", split_axis=0, concat_axis=1, tiled=True),
        lax.all_to_all(value_back, "head", split_axis=0, concat_axis=1, tiled=True),
    )
    text_query_grad = rotate(text_query_sum, text_place, text_place, -1.0).astype(jnp.bfloat16)
    text_key_grad = rotate(text_key_sum, text_place, text_place, -1.0).astype(jnp.bfloat16)
    text_value_grad = text_value_sum.astype(jnp.bfloat16)
    return (
        slab_query_grad,
        image_key_grad,
        image_value_grad,
        text_query_grad,
        text_key_grad,
        text_value_grad,
    )


def solution(mesh):
    in_specs = (
        P(("rep", "blk", "head"), None),
        P(("rep", "blk", "head"), None),
        P(("rep", "blk", "head"), None),
        P(("rep", "blk"), "head"),
        P(("rep", "blk", "head"), None),
        P(("rep", "blk", "head"), None),
        P("rep", "head"),
        P("rep", "head"),
        P("rep", "head"),
        P("rep", "head"),
        P("rep", "head"),
        P("rep", "head"),
        P("rep"),
        P("rep"),
    )
    out_specs = (
        P(("rep", "blk", "head"), None),
        P(("rep", "blk", "head"), None),
        P(("rep", "blk", "head"), None),
        P("rep", "head"),
        P("rep", "head"),
        P("rep", "head"),
    )
    return jax.shard_map(
        on_device, mesh=mesh, in_specs=in_specs, out_specs=out_specs, check_vma=False
    )
```

profile of v0, /device:TPU:1, one launch (start us, length us, event | category | flops | bytes accessed | tf_op | source)
XLA Modules:
  0.0 818.7 jit_solution(5279995481750665881)
XLA Ops:
  7.8 13.1 %all-to-all-start = ((bf16[8,8,384]{2,0,1:T(8,128)(2,1)}), bf16[8,8,384]{2,0,1:T(8,128)(2,1)}, u32[]{:S(2)}, u32[]{:S(2)}) async-start(bf16[8,8,384]{2,0,1:T(8,128)(2,1)} %bitcast.332), calls=%async_computation | async-start | bytes 98304 | tf_op jit(solution)/shard_map/all_to_all | solution.py:95
  35.3 9.4 %all-to-all-start.2 = ((bf16[8,8,384]{2,0,1:T(8,128)(2,1)}), bf16[8,8,384]{2,0,1:T(8,128)(2,1)S(1)}, u32[]{:S(2)}, u32[]{:S(2)}) async-start(bf16[8,8,384]{2,0,1:T(8,128)(2,1)} %bitcast.22), calls=%async_computation.2 | async-start | bytes 98304 | tf_op jit(solution)/shard_map/all_to_all | solution.py:96
  45.5 8.9 %all-to-all-done.2 = bf16[8,8,384]{2,0,1:T(8,128)(2,1)S(1)} async-done(((bf16[8,8,384]{2,0,1:T(8,128)(2,1)}), bf16[8,8,384]{2,0,1:T(8,128)(2,1)S(1)}, u32[]{:S(2)}, u32[]{:S(2)}) %all-to-all-start.2) | async-done | bytes 49184 | tf_op jit(solution)/shard_map/all_to_all | solution.py:96
  57.9 9.5 %all-to-all-done.1 = bf16[8,8,384]{2,0,1:T(8,128)(2,1)S(1)} async-done(((bf16[8,8,384]{2,0,1:T(8,128)(2,1)}), bf16[8,8,384]{2,0,1:T(8,128)(2,1)S(1)}, u32[]{:S(2)}, u32[]{:S(2)}) %all-to-all-start.1) | async-done | bytes 49184 | tf_op jit(solution)/shard_map/all_to_all | solution.py:97
  74.8 7.0 all-to-all-done.3
  81.8 5.6 all-to-all-start.4
  88.7 9.7 %all-to-all-done.4 = bf16[32,8,384]{2,0,1:T(8,128)(2,1)S(1)} async-done(((bf16[32,8,384]{2,0,1:T(8,128)(2,1)}), bf16[32,8,384]{2,0,1:T(8,128)(2,1)S(1)}, u32[]{:S(2)}, u32[]{:S(2)}) %all-to-all-start.4) | async-done | bytes 196640 | tf_op jit(solution)/shard_map/all_to_all | solution.py:99
  100.4 537.5 %while.22 = (s32[]{:T(128)}, bf16[64,384]{1,0:T(8,128)(2,1)S(1)}, bf16[64,384]{1,0:T(8,128)(2,1)S(1)}, f32[64,3]{0,1:T(4,128)S(1)}, f32[64,3]{0,1:T(4,128)S(1)},...) while((s32[]{:T(128)}, bf16[64,384]{1,0:T(8,128)(2,1)S(1)}, ...), condition=%wide.region_3.4_spmd, body=%wide.region_2.3_spmd.sunk | while | flops 126959616 | bytes 10436093 | solution.py:186
  100.4 7.5 collective-permute-start
  135.2 4.3 collective-permute-start
  153.3 5.3 collective-permute-start.7
  167.3 4.3 collective-permute-start
  185.6 6.4 collective-permute-start.7
  200.7 4.3 collective-permute-start
  218.3 6.4 collective-permute-start.7
  233.4 4.3 collective-permute-start
  244.4 5.7 collective-permute-start.8
  253.3 6.4 collective-permute-start.7
  268.4 4.3 collective-permute-start
  279.2 4.7 collective-permute-start.8
  287.0 6.4 collective-permute-start.7
  302.1 4.3 collective-permute-start
  312.9 4.4 collective-permute-start.8
  320.5 6.4 collective-permute-start.7
  335.6 4.3 collective-permute-start
  353.2 6.4 collective-permute-start.7
  368.3 4.3 collective-permute-start
  379.2 5.7 collective-permute-start.8
  388.1 6.4 collective-permute-start.7
  403.2 4.3 collective-permute-start
  414.0 4.7 collective-permute-start.8
  421.8 6.4 collective-permute-start.7
  436.9 4.3 collective-permute-start
  447.7 4.4 collective-permute-start.8
  455.3 6.4 collective-permute-start.7
  488.0 6.4 collective-permute-start.7
  514.0 5.7 collective-permute-start.8
  523.0 6.4 collective-permute-start.7
  548.8 4.7 collective-permute-start.8
  556.7 6.4 collective-permute-start.7
  582.5 4.4 collective-permute-start.8
  590.1 6.4 collective-permute-start.7
  622.8 6.4 collective-permute-start.7
  639.6 4.3 all-to-all-start.5
  647.9 5.6 all-to-all-done.5
  657.3 129.7 %all-reduce.3.cloned.1.call-done = (f32[256,384]{0,1:T(8,128)}, f32[256,384]{0,1:T(8,128)}, f32[256,384]{1,0:T(8,128)}) async-done(((f32[256,384]{0,1:T(8,128)}, f32[256,384]{0,1:T(8,128)}, f32[256,384]{1,0:T(8,128)}), (f32[256,384]{0,1:T(8,128)}, f32[256,384]{0,1:T(8,128)}, f32[256,384]{1,0:T(8,128)})) %all-reduce.3.cloned.1.call-update) | async-done | bytes 1179664 | tf_op jit(solution)/shard_map/psum | solution.py:147
  789.7 9.8 %all-to-all-start.7 = ((bf16[8,32,384]{2,1,0:T(8,128)(2,1)}), bf16[8,32,384]{2,1,0:T(8,128)(2,1)S(1)}, u32[]{:S(2)}, u32[]{:S(2)}) async-start(bf16[8,32,384]{2,1,0:T(8,128)(2,1)} %bitcast.49), calls=%async_computation.7 | async-start | bytes 393216 | tf_op jit(solution)/shard_map/all_to_all | solution.py:196
  803.4 7.1 all-to-all-done.7
  (661 shorter events, 389.3 us)
Async XLA Ops:
  7.8 27.4 %all-to-all-start = ((bf16[8,8,384]{2,0,1:T(8,128)(2,1)}), bf16[8,8,384]{2,0,1:T(8,128)(2,1)}, u32[]{:S(2)}, u32[]{:S(2)}) async-start(bf16[8,8,384]{2,0,1:T(8,128)(2,1)} %bitcast.332), calls=%async_computation | async-start | bytes 98304 | tf_op jit(solution)/shard_map/all_to_all | solution.py:95
  35.3 19.1 %all-to-all-start.2 = ((bf16[8,8,384]{2,0,1:T(8,128)(2,1)}), bf16[8,8,384]{2,0,1:T(8,128)(2,1)S(1)}, u32[]{:S(2)}, u32[]{:S(2)}) async-start(bf16[8,8,384]{2,0,1:T(8,128)(2,1)} %bitcast.22), calls=%async_computation.2 | async-start | bytes 98304 | tf_op jit(solution)/shard_map/all_to_all | solution.py:96
  100.4 24.5 %collective-permute-start = (bf16[64,384]{1,0:T(8,128)(2,1)S(1)}, bf16[64,384]{1,0:T(8,128)(2,1)S(1)}, u32[]{:S(2)}, u32[]{:S(2)}) collective-permute-start(bf16[64,384]{1,0:T(8,128)(2,1)S(1)} %get-tuple-element.267), channel_id=1, source_target_pairs={{0,16},{16,32},{32,48},{48,64},{64,80},{80,96},{96,112},{112,128},... | collective-permute-start | bytes 147464 | tf_op jit(solution)/shard_map/while/body/eval_jaxpr/ppermute | solution.py:13
  135.2 23.4 %collective-permute-start = (bf16[64,384]{1,0:T(8,128)(2,1)S(1)}, bf16[64,384]{1,0:T(8,128)(2,1)S(1)}, u32[]{:S(2)}, u32[]{:S(2)}) collective-permute-start(bf16[64,384]{1,0:T(8,128)(2,1)S(1)} %get-tuple-element.267), channel_id=1, source_target_pairs={{0,16},{16,32},{32,48},{48,64},{64,80},{80,96},{96,112},{112,128},... | collective-permute-start | bytes 147464 | tf_op jit(solution)/shard_map/while/body/eval_jaxpr/ppermute | solution.py:13
  139.5 19.3 %collective-permute-start.2 = (bf16[64,384]{1,0:T(8,128)(2,1)S(1)}, bf16[64,384]{1,0:T(8,128)(2,1)S(1)}, u32[]{:S(2)}, u32[]{:S(2)}) collective-permute-start(bf16[64,384]{1,0:T(8,128)(2,1)S(1)} %get-tuple-element.268), channel_id=1, source_target_pairs={{0,16},{16,32},{32,48},{48,64},{64,80},{80,96},{96,112},{112,128},... | collective-permute-start | bytes 147464 | tf_op jit(solution)/shard_map/while/body/eval_jaxpr/ppermute | solution.py:13
  167.3 24.8 %collective-permute-start = (bf16[64,384]{1,0:T(8,128)(2,1)S(1)}, bf16[64,384]{1,0:T(8,128)(2,1)S(1)}, u32[]{:S(2)}, u32[]{:S(2)}) collective-permute-start(bf16[64,384]{1,0:T(8,128)(2,1)S(1)} %get-tuple-element.267), channel_id=1, source_target_pairs={{0,16},{16,32},{32,48},{48,64},{64,80},{80,96},{96,112},{112,128},... | collective-permute-start | bytes 147464 | tf_op jit(solution)/shard_map/while/body/eval_jaxpr/ppermute | solution.py:13
  171.6 20.7 %collective-permute-start.2 = (bf16[64,384]{1,0:T(8,128)(2,1)S(1)}, bf16[64,384]{1,0:T(8,128)(2,1)S(1)}, u32[]{:S(2)}, u32[]{:S(2)}) collective-permute-start(bf16[64,384]{1,0:T(8,128)(2,1)S(1)} %get-tuple-element.268), channel_id=1, source_target_pairs={{0,16},{16,32},{32,48},{48,64},{64,80},{80,96},{96,112},{112,128},... | collective-permute-start | bytes 147464 | tf_op jit(solution)/shard_map/while/body/eval_jaxpr/ppermute | solution.py:13
  200.7 24.0 %collective-permute-start = (bf16[64,384]{1,0:T(8,128)(2,1)S(1)}, bf16[64,384]{1,0:T(8,128)(2,1)S(1)}, u32[]{:S(2)}, u32[]{:S(2)}) collective-permute-start(bf16[64,384]{1,0:T(8,128)(2,1)S(1)} %get-tuple-element.267), channel_id=1, source_target_pairs={{0,16},{16,32},{32,48},{48,64},{64,80},{80,96},{96,112},{112,128},... | collective-permute-start | bytes 147464 | tf_op jit(solution)/shard_map/while/body/eval_jaxpr/ppermute | solution.py:13
  205.0 19.9 %collective-permute-start.2 = (bf16[64,384]{1,0:T(8,128)(2,1)S(1)}, bf16[64,384]{1,0:T(8,128)(2,1)S(1)}, u32[]{:S(2)}, u32[]{:S(2)}) collective-permute-start(bf16[64,384]{1,0:T(8,128)(2,1)S(1)} %get-tuple-element.268), channel_id=1, source_target_pairs={{0,16},{16,32},{32,48},{48,64},{64,80},{80,96},{96,112},{112,128},... | collective-permute-start | bytes 147464 | tf_op jit(solution)/shard_map/while/body/eval_jaxpr/ppermute | solution.py:13
  211.5 18.4 %collective-permute-start.8 = (f32[64,384]{1,0:T(8,128)S(1)}, f32[64,384]{1,0:T(8,128)S(1)}, u32[]{:S(2)}, u32[]{:S(2)}) collective-permute-start(f32[64,384]{1,0:T(8,128)S(1)} %bitcast_add_fusion.12), channel_id=1, source_target_pairs={{0,16},{16,32},{32,48},{48,64},{64,80},{80,96},{96,112},{112,128},... | collective-permute-start | bytes 294920 | tf_op jit(solution)/shard_map/while/body/eval_jaxpr/ppermute | solution.py:13
  233.4 26.3 %collective-permute-start = (bf16[64,384]{1,0:T(8,128)(2,1)S(1)}, bf16[64,384]{1,0:T(8,128)(2,1)S(1)}, u32[]{:S(2)}, u32[]{:S(2)}) collective-permute-start(bf16[64,384]{1,0:T(8,128)(2,1)S(1)} %get-tuple-element.267), channel_id=1, source_target_pairs={{0,16},{16,32},{32,48},{48,64},{64,80},{80,96},{96,112},{112,128},... | collective-permute-start | bytes 147464 | tf_op jit(solution)/shard_map/while/body/eval_jaxpr/ppermute | solution.py:13
  237.7 22.2 %collective-permute-start.2 = (bf16[64,384]{1,0:T(8,128)(2,1)S(1)}, bf16[64,384]{1,0:T(8,128)(2,1)S(1)}, u32[]{:S(2)}, u32[]{:S(2)}) collective-permute-start(bf16[64,384]{1,0:T(8,128)(2,1)S(1)} %get-tuple-element.268), channel_id=1, source_target_pairs={{0,16},{16,32},{32,48},{48,64},{64,80},{80,96},{96,112},{112,128},... | collective-permute-start | bytes 147464 | tf_op jit(solution)/shard_map/while/body/eval_jaxpr/ppermute | solution.py:13
  244.4 20.4 %collective-permute-start.8 = (f32[64,384]{1,0:T(8,128)S(1)}, f32[64,384]{1,0:T(8,128)S(1)}, u32[]{:S(2)}, u32[]{:S(2)}) collective-permute-start(f32[64,384]{1,0:T(8,128)S(1)} %bitcast_add_fusion.12), channel_id=1, source_target_pairs={{0,16},{16,32},{32,48},{48,64},{64,80},{80,96},{96,112},{112,128},... | collective-permute-start | bytes 294920 | tf_op jit(solution)/shard_map/while/body/eval_jaxpr/ppermute | solution.py:13
  268.4 25.1 %collective-permute-start = (bf16[64,384]{1,0:T(8,128)(2,1)S(1)}, bf16[64,384]{1,0:T(8,128)(2,1)S(1)}, u32[]{:S(2)}, u32[]{:S(2)}) collective-permute-start(bf16[64,384]{1,0:T(8,128)(2,1)S(1)} %get-tuple-element.267), channel_id=1, source_target_pairs={{0,16},{16,32},{32,48},{48,64},{64,80},{80,96},{96,112},{112,128},... | collective-permute-start | bytes 147464 | tf_op jit(solution)/shard_map/while/body/eval_jaxpr/ppermute | solution.py:13
  272.7 21.0 %collective-permute-start.2 = (bf16[64,384]{1,0:T(8,128)(2,1)S(1)}, bf16[64,384]{1,0:T(8,128)(2,1)S(1)}, u32[]{:S(2)}, u32[]{:S(2)}) collective-permute-start(bf16[64,384]{1,0:T(8,128)(2,1)S(1)} %get-tuple-element.268), channel_id=1, source_target_pairs={{0,16},{16,32},{32,48},{48,64},{64,80},{80,96},{96,112},{112,128},... | collective-permute-start | bytes 147464 | tf_op jit(solution)/shard_map/while/body/eval_jaxpr/ppermute | solution.py:13
  279.2 19.4 %collective-permute-start.8 = (f32[64,384]{1,0:T(8,128)S(1)}, f32[64,384]{1,0:T(8,128)S(1)}, u32[]{:S(2)}, u32[]{:S(2)}) collective-permute-start(f32[64,384]{1,0:T(8,128)S(1)} %bitcast_add_fusion.12), channel_id=1, source_target_pairs={{0,16},{16,32},{32,48},{48,64},{64,80},{80,96},{96,112},{112,128},... | collective-permute-start | bytes 294920 | tf_op jit(solution)/shard_map/while/body/eval_jaxpr/ppermute | solution.py:13
  302.1 24.8 %collective-permute-start = (bf16[64,384]{1,0:T(8,128)(2,1)S(1)}, bf16[64,384]{1,0:T(8,128)(2,1)S(1)}, u32[]{:S(2)}, u32[]{:S(2)}) collective-permute-start(bf16[64,384]{1,0:T(8,128)(2,1)S(1)} %get-tuple-element.267), channel_id=1, source_target_pairs={{0,16},{16,32},{32,48},{48,64},{64,80},{80,96},{96,112},{112,128},... | collective-permute-start | bytes 147464 | tf_op jit(solution)/shard_map/while/body/eval_jaxpr/ppermute | solution.py:13
  306.4 20.7 %collective-permute-start.2 = (bf16[64,384]{1,0:T(8,128)(2,1)S(1)}, bf16[64,384]{1,0:T(8,128)(2,1)S(1)}, u32[]{:S(2)}, u32[]{:S(2)}) collective-permute-start(bf16[64,384]{1,0:T(8,128)(2,1)S(1)} %get-tuple-element.268), channel_id=1, source_target_pairs={{0,16},{16,32},{32,48},{48,64},{64,80},{80,96},{96,112},{112,128},... | collective-permute-start | bytes 147464 | tf_op jit(solution)/shard_map/while/body/eval_jaxpr/ppermute | solution.py:13
  312.9 19.1 %collective-permute-start.8 = (f32[64,384]{1,0:T(8,128)S(1)}, f32[64,384]{1,0:T(8,128)S(1)}, u32[]{:S(2)}, u32[]{:S(2)}) collective-permute-start(f32[64,384]{1,0:T(8,128)S(1)} %bitcast_add_fusion.12), channel_id=1, source_target_pairs={{0,16},{16,32},{32,48},{48,64},{64,80},{80,96},{96,112},{112,128},... | collective-permute-start | bytes 294920 | tf_op jit(solution)/shard_map/while/body/eval_jaxpr/ppermute | solution.py:13
  335.6 24.0 %collective-permute-start = (bf16[64,384]{1,0:T(8,128)(2,1)S(1)}, bf16[64,384]{1,0:T(8,128)(2,1)S(1)}, u32[]{:S(2)}, u32[]{:S(2)}) collective-permute-start(bf16[64,384]{1,0:T(8,128)(2,1)S(1)} %get-tuple-element.267), channel_id=1, source_target_pairs={{0,16},{16,32},{32,48},{48,64},{64,80},{80,96},{96,112},{112,128},... | collective-permute-start | bytes 147464 | tf_op jit(solution)/shard_map/while/body/eval_jaxpr/ppermute | solution.py:13
  339.9 19.9 %collective-permute-start.2 = (bf16[64,384]{1,0:T(8,128)(2,1)S(1)}, bf16[64,384]{1,0:T(8,128)(2,1)S(1)}, u32[]{:S(2)}, u32[]{:S(2)}) collective-permute-start(bf16[64,384]{1,0:T(8,128)(2,1)S(1)} %get-tuple-element.268), channel_id=1, source_target_pairs={{0,16},{16,32},{32,48},{48,64},{64,80},{80,96},{96,112},{112,128},... | collective-permute-start | bytes 147464 | tf_op jit(solution)/shard_map/while/body/eval_jaxpr/ppermute | solution.py:13
  346.3 18.4 %collective-permute-start.8 = (f32[64,384]{1,0:T(8,128)S(1)}, f32[64,384]{1,0:T(8,128)S(1)}, u32[]{:S(2)}, u32[]{:S(2)}) collective-permute-start(f32[64,384]{1,0:T(8,128)S(1)} %bitcast_add_fusion.12), channel_id=1, source_target_pairs={{0,16},{16,32},{32,48},{48,64},{64,80},{80,96},{96,112},{112,128},... | collective-permute-start | bytes 294920 | tf_op jit(solution)/shard_map/while/body/eval_jaxpr/ppermute | solution.py:13
  368.3 26.3 %collective-permute-start = (bf16[64,384]{1,0:T(8,128)(2,1)S(1)}, bf16[64,384]{1,0:T(8,128)(2,1)S(1)}, u32[]{:S(2)}, u32[]{:S(2)}) collective-permute-start(bf16[64,384]{1,0:T(8,128)(2,1)S(1)} %get-tuple-element.267), channel_id=1, source_target_pairs={{0,16},{16,32},{32,48},{48,64},{64,80},{80,96},{96,112},{112,128},... | collective-permute-start | bytes 147464 | tf_op jit(solution)/shard_map/while/body/eval_jaxpr/ppermute | solution.py:13
  372.6 22.2 %collective-permute-start.2 = (bf16[64,384]{1,0:T(8,128)(2,1)S(1)}, bf16[64,384]{1,0:T(8,128)(2,1)S(1)}, u32[]{:S(2)}, u32[]{:S(2)}) collective-permute-start(bf16[64,384]{1,0:T(8,128)(2,1)S(1)} %get-tuple-element.268), channel_id=1, source_target_pairs={{0,16},{16,32},{32,48},{48,64},{64,80},{80,96},{96,112},{112,128},... | collective-permute-start | bytes 147464 | tf_op jit(solution)/shard_map/while/body/eval_jaxpr/ppermute | solution.py:13
  379.2 20.4 %collective-permute-start.8 = (f32[64,384]{1,0:T(8,128)S(1)}, f32[64,384]{1,0:T(8,128)S(1)}, u32[]{:S(2)}, u32[]{:S(2)}) collective-permute-start(f32[64,384]{1,0:T(8,128)S(1)} %bitcast_add_fusion.12), channel_id=1, source_target_pairs={{0,16},{16,32},{32,48},{48,64},{64,80},{80,96},{96,112},{112,128},... | collective-permute-start | bytes 294920 | tf_op jit(solution)/shard_map/while/body/eval_jaxpr/ppermute | solution.py:13
  403.2 25.1 %collective-permute-start = (bf16[64,384]{1,0:T(8,128)(2,1)S(1)}, bf16[64,384]{1,0:T(8,128)(2,1)S(1)}, u32[]{:S(2)}, u32[]{:S(2)}) collective-permute-start(bf16[64,384]{1,0:T(8,128)(2,1)S(1)} %get-tuple-element.267), channel_id=1, source_target_pairs={{0,16},{16,32},{32,48},{48,64},{64,80},{80,96},{96,112},{112,128},... | collective-permute-start | bytes 147464 | tf_op jit(solution)/shard_map/while/body/eval_jaxpr/ppermute | solution.py:13
  407.5 21.0 %collective-permute-start.2 = (bf16[64,384]{1,0:T(8,128)(2,1)S(1)}, bf16[64,384]{1,0:T(8,128)(2,1)S(1)}, u32[]{:S(2)}, u32[]{:S(2)}) collective-permute-start(bf16[64,384]{1,0:T(8,128)(2,1)S(1)} %get-tuple-element.268), channel_id=1, source_target_pairs={{0,16},{16,32},{32,48},{48,64},{64,80},{80,96},{96,112},{112,128},... | collective-permute-start | bytes 147464 | tf_op jit(solution)/shard_map/while/body/eval_jaxpr/ppermute | solution.py:13
  414.0 19.4 %collective-permute-start.8 = (f32[64,384]{1,0:T(8,128)S(1)}, f32[64,384]{1,0:T(8,128)S(1)}, u32[]{:S(2)}, u32[]{:S(2)}) collective-permute-start(f32[64,384]{1,0:T(8,128)S(1)} %bitcast_add_fusion.12), channel_id=1, source_target_pairs={{0,16},{16,32},{32,48},{48,64},{64,80},{80,96},{96,112},{112,128},... | collective-permute-start | bytes 294920 | tf_op jit(solution)/shard_map/while/body/eval_jaxpr/ppermute | solution.py:13
  436.9 24.8 %collective-permute-start = (bf16[64,384]{1,0:T(8,128)(2,1)S(1)}, bf16[64,384]{1,0:T(8,128)(2,1)S(1)}, u32[]{:S(2)}, u32[]{:S(2)}) collective-permute-start(bf16[64,384]{1,0:T(8,128)(2,1)S(1)} %get-tuple-element.267), channel_id=1, source_target_pairs={{0,16},{16,32},{32,48},{48,64},{64,80},{80,96},{96,112},{112,128},... | collective-permute-start | bytes 147464 | tf_op jit(solution)/shard_map/while/body/eval_jaxpr/ppermute | solution.py:13
  441.2 20.7 %collective-permute-start.2 = (bf16[64,384]{1,0:T(8,128)(2,1)S(1)}, bf16[64,384]{1,0:T(8,128)(2,1)S(1)}, u32[]{:S(2)}, u32[]{:S(2)}) collective-permute-start(bf16[64,384]{1,0:T(8,128)(2,1)S(1)} %get-tuple-element.268), channel_id=1, source_target_pairs={{0,16},{16,32},{32,48},{48,64},{64,80},{80,96},{96,112},{112,128},... | collective-permute-start | bytes 147464 | tf_op jit(solution)/shard_map/while/body/eval_jaxpr/ppermute | solution.py:13
  447.7 19.1 %collective-permute-start.8 = (f32[64,384]{1,0:T(8,128)S(1)}, f32[64,384]{1,0:T(8,128)S(1)}, u32[]{:S(2)}, u32[]{:S(2)}) collective-permute-start(f32[64,384]{1,0:T(8,128)S(1)} %bitcast_add_fusion.12), channel_id=1, source_target_pairs={{0,16},{16,32},{32,48},{48,64},{64,80},{80,96},{96,112},{112,128},... | collective-permute-start | bytes 294920 | tf_op jit(solution)/shard_map/while/body/eval_jaxpr/ppermute | solution.py:13
  470.4 24.0 %collective-permute-start = (bf16[64,384]{1,0:T(8,128)(2,1)S(1)}, bf16[64,384]{1,0:T(8,128)(2,1)S(1)}, u32[]{:S(2)}, u32[]{:S(2)}) collective-permute-start(bf16[64,384]{1,0:T(8,128)(2,1)S(1)} %get-tuple-element.267), channel_id=1, source_target_pairs={{0,16},{16,32},{32,48},{48,64},{64,80},{80,96},{96,112},{112,128},... | collective-permute-start | bytes 147464 | tf_op jit(solution)/shard_map/while/body/eval_jaxpr/ppermute | solution.py:13
  474.7 19.9 %collective-permute-start.2 = (bf16[64,384]{1,0:T(8,128)(2,1)S(1)}, bf16[64,384]{1,0:T(8,128)(2,1)S(1)}, u32[]{:S(2)}, u32[]{:S(2)}) collective-permute-start(bf16[64,384]{1,0:T(8,128)(2,1)S(1)} %get-tuple-element.268), channel_id=1, source_target_pairs={{0,16},{16,32},{32,48},{48,64},{64,80},{80,96},{96,112},{112,128},... | collective-permute-start | bytes 147464 | tf_op jit(solution)/shard_map/while/body/eval_jaxpr/ppermute | solution.py:13
  481.2 18.4 %collective-permute-start.8 = (f32[64,384]{1,0:T(8,128)S(1)}, f32[64,384]{1,0:T(8,128)S(1)}, u32[]{:S(2)}, u32[]{:S(2)}) collective-permute-start(f32[64,384]{1,0:T(8,128)S(1)} %bitcast_add_fusion.12), channel_id=1, source_target_pairs={{0,16},{16,32},{32,48},{48,64},{64,80},{80,96},{96,112},{112,128},... | collective-permute-start | bytes 294920 | tf_op jit(solution)/shard_map/while/body/eval_jaxpr/ppermute | solution.py:13
  503.1 26.3 %collective-permute-start = (bf16[64,384]{1,0:T(8,128)(2,1)S(1)}, bf16[64,384]{1,0:T(8,128)(2,1)S(1)}, u32[]{:S(2)}, u32[]{:S(2)}) collective-permute-start(bf16[64,384]{1,0:T(8,128)(2,1)S(1)} %get-tuple-element.267), channel_id=1, source_target_pairs={{0,16},{16,32},{32,48},{48,64},{64,80},{80,96},{96,112},{112,128},... | collective-permute-start | bytes 147464 | tf_op jit(solution)/shard_map/while/body/eval_jaxpr/ppermute | solution.py:13
  507.4 22.2 %collective-permute-start.2 = (bf16[64,384]{1,0:T(8,128)(2,1)S(1)}, bf16[64,384]{1,0:T(8,128)(2,1)S(1)}, u32[]{:S(2)}, u32[]{:S(2)}) collective-permute-start(bf16[64,384]{1,0:T(8,128)(2,1)S(1)} %get-tuple-element.268), channel_id=1, source_target_pairs={{0,16},{16,32},{32,48},{48,64},{64,80},{80,96},{96,112},{112,128},... | collective-permute-start | bytes 147464 | tf_op jit(solution)/shard_map/while/body/eval_jaxpr/ppermute | solution.py:13
  514.0 20.4 %collective-permute-start.8 = (f32[64,384]{1,0:T(8,128)S(1)}, f32[64,384]{1,0:T(8,128)S(1)}, u32[]{:S(2)}, u32[]{:S(2)}) collective-permute-start(f32[64,384]{1,0:T(8,128)S(1)} %bitcast_add_fusion.12), channel_id=1, source_target_pairs={{0,16},{16,32},{32,48},{48,64},{64,80},{80,96},{96,112},{112,128},... | collective-permute-start | bytes 294920 | tf_op jit(solution)/shard_map/while/body/eval_jaxpr/ppermute | solution.py:13
  538.0 25.1 %collective-permute-start = (bf16[64,384]{1,0:T(8,128)(2,1)S(1)}, bf16[64,384]{1,0:T(8,128)(2,1)S(1)}, u32[]{:S(2)}, u32[]{:S(2)}) collective-permute-start(bf16[64,384]{1,0:T(8,128)(2,1)S(1)} %get-tuple-element.267), channel_id=1, source_target_pairs={{0,16},{16,32},{32,48},{48,64},{64,80},{80,96},{96,112},{112,128},... | collective-permute-start | bytes 147464 | tf_op jit(solution)/shard_map/while/body/eval_jaxpr/ppermute | solution.py:13
  542.3 21.0 %collective-permute-start.2 = (bf16[64,384]{1,0:T(8,128)(2,1)S(1)}, bf16[64,384]{1,0:T(8,128)(2,1)S(1)}, u32[]{:S(2)}, u32[]{:S(2)}) collective-permute-start(bf16[64,384]{1,0:T(8,128)(2,1)S(1)} %get-tuple-element.268), channel_id=1, source_target_pairs={{0,16},{16,32},{32,48},{48,64},{64,80},{80,96},{96,112},{112,128},... | collective-permute-start | bytes 147464 | tf_op jit(solution)/shard_map/while/body/eval_jaxpr/ppermute | solution.py:13
  548.8 19.4 %collective-permute-start.8 = (f32[64,384]{1,0:T(8,128)S(1)}, f32[64,384]{1,0:T(8,128)S(1)}, u32[]{:S(2)}, u32[]{:S(2)}) collective-permute-start(f32[64,384]{1,0:T(8,128)S(1)} %bitcast_add_fusion.12), channel_id=1, source_target_pairs={{0,16},{16,32},{32,48},{48,64},{64,80},{80,96},{96,112},{112,128},... | collective-permute-start | bytes 294920 | tf_op jit(solution)/shard_map/while/body/eval_jaxpr/ppermute | solution.py:13
  571.8 24.8 %collective-permute-start = (bf16[64,384]{1,0:T(8,128)(2,1)S(1)}, bf16[64,384]{1,0:T(8,128)(2,1)S(1)}, u32[]{:S(2)}, u32[]{:S(2)}) collective-permute-start(bf16[64,384]{1,0:T(8,128)(2,1)S(1)} %get-tuple-element.267), channel_id=1, source_target_pairs={{0,16},{16,32},{32,48},{48,64},{64,80},{80,96},{96,112},{112,128},... | collective-permute-start | bytes 147464 | tf_op jit(solution)/shard_map/while/body/eval_jaxpr/ppermute | solution.py:13
  576.1 20.7 %collective-permute-start.2 = (bf16[64,384]{1,0:T(8,128)(2,1)S(1)}, bf16[64,384]{1,0:T(8,128)(2,1)S(1)}, u32[]{:S(2)}, u32[]{:S(2)}) collective-permute-start(bf16[64,384]{1,0:T(8,128)(2,1)S(1)} %get-tuple-element.268), channel_id=1, source_target_pairs={{0,16},{16,32},{32,48},{48,64},{64,80},{80,96},{96,112},{112,128},... | collective-permute-start | bytes 147464 | tf_op jit(solution)/shard_map/while/body/eval_jaxpr/ppermute | solution.py:13
  582.5 19.1 %collective-permute-start.8 = (f32[64,384]{1,0:T(8,128)S(1)}, f32[64,384]{1,0:T(8,128)S(1)}, u32[]{:S(2)}, u32[]{:S(2)}) collective-permute-start(f32[64,384]{1,0:T(8,128)S(1)} %bitcast_add_fusion.12), channel_id=1, source_target_pairs={{0,16},{16,32},{32,48},{48,64},{64,80},{80,96},{96,112},{112,128},... | collective-permute-start | bytes 294920 | tf_op jit(solution)/shard_map/while/body/eval_jaxpr/ppermute | solution.py:13
  605.2 24.0 %collective-permute-start = (bf16[64,384]{1,0:T(8,128)(2,1)S(1)}, bf16[64,384]{1,0:T(8,128)(2,1)S(1)}, u32[]{:S(2)}, u32[]{:S(2)}) collective-permute-start(bf16[64,384]{1,0:T(8,128)(2,1)S(1)} %get-tuple-element.267), channel_id=1, source_target_pairs={{0,16},{16,32},{32,48},{48,64},{64,80},{80,96},{96,112},{112,128},... | collective-permute-start | bytes 147464 | tf_op jit(solution)/shard_map/while/body/eval_jaxpr/ppermute | solution.py:13
  609.5 19.9 %collective-permute-start.2 = (bf16[64,384]{1,0:T(8,128)(2,1)S(1)}, bf16[64,384]{1,0:T(8,128)(2,1)S(1)}, u32[]{:S(2)}, u32[]{:S(2)}) collective-permute-start(bf16[64,384]{1,0:T(8,128)(2,1)S(1)} %get-tuple-element.268), channel_id=1, source_target_pairs={{0,16},{16,32},{32,48},{48,64},{64,80},{80,96},{96,112},{112,128},... | collective-permute-start | bytes 147464 | tf_op jit(solution)/shard_map/while/body/eval_jaxpr/ppermute | solution.py:13
  643.9 143.1 %all-reduce.3.cloned.1.call-start = ((), (), s32[]{:S(2)}) async-start(), calls=%async_computation.8 | async-start | bytes 2359296 | tf_op jit(solution)/shard_map/psum | solution.py:147
  653.5 136.1 %all-to-all-start.6 = ((bf16[8,32,384]{2,1,0:T(8,128)(2,1)}), bf16[8,32,384]{2,1,0:T(8,128)(2,1)S(1)}, u32[]{:S(2)}, u32[]{:S(2)}) async-start(bf16[8,32,384]{2,1,0:T(8,128)(2,1)} %convert_element_type.184), calls=%async_computation.6 | async-start | bytes 393216 | tf_op jit(solution)/shard_map/all_to_all | solution.py:195
  789.7 20.8 %all-to-all-start.7 = ((bf16[8,32,384]{2,1,0:T(8,128)(2,1)}), bf16[8,32,384]{2,1,0:T(8,128)(2,1)S(1)}, u32[]{:S(2)}, u32[]{:S(2)}) async-start(bf16[8,32,384]{2,1,0:T(8,128)(2,1)} %bitcast.49), calls=%async_computation.7 | async-start | bytes 393216 | tf_op jit(solution)/shard_map/all_to_all | solution.py:196
  (144 other events, 1435.6 us)
Sparse Core Ops, SparseCore 0:
  648.3 138.6 all-reduce.2
where the time goes:
time: 827 us; the launch traced here: 819 us
  starting transfers between devices  525 us (63%)
  waiting for transfers between devices  202 us (24%)
  matrix products  39.6 us (5%)
  local copies, waits for them, and re-layouts  20.1 us (2%)
  between operations  16 us (2%)
  other arithmetic  12.7 us (2%)
    ppermute x160, starting transfers between devices, from_behind(): return lax.ppermute(value, axis, pairs)  472 us
    psum x1, waiting for transfers between devices, on_device(): lax.psum((text_query_part, text_key_part, text_value_part), 'blk')  130 us
    ppermute x160, waiting for transfers between devices, from_behind(): return lax.ppermute(value, axis, pairs)  23.6 us
  transfers between devices with their start and end apart: 169, of which 23 were waited for; matrix products, arithmetic and copies ran while one was open for 8% of the time, Pallas kernels for 0%

commit v1 on v0

v1 whole, which is shorter than its diff:
```python
import functools

import jax
import jax.numpy as jnp
import numpy as np
from jax import lax
from jax.experimental import pallas as pl
from jax.experimental.pallas import tpu as pltpu
from jax.sharding import PartitionSpec as P

HEAD_DIM = 128
FACTOR = HEAD_DIM ** (-0.5)
NZ = 8
NB = 16
HD = 3
W = HD * HEAD_DIM
TXT = 256
HALF = TXT // 2
ROWS = 64
KEYS = 256
SLAB_Q = NB * ROWS
SILENT = 1e30
BF = jnp.bfloat16
F32 = jnp.float32
MESH = pl.DeviceIdType.MESH


def tables():
    place = np.arange(512, dtype=np.float64)[:, None]
    frequency = 10000.0 ** (-np.arange(32, dtype=np.float64) / 32)
    angles = np.tile(place * frequency[None, :], (1, 4))
    sign = np.where(np.arange(128) < 64, -1.0, 1.0)
    return np.cos(angles).astype(np.float32), (np.sin(angles) * sign).astype(np.float32)


def nt(a, b):
    return lax.dot_general(a, b, (((1,), (1,)), ((), ())), preferred_element_type=F32)


def nn(a, b):
    return lax.dot_general(a, b, (((1,), (0,)), ((), ())), preferred_element_type=F32)


def tn(a, b):
    return lax.dot_general(a, b, (((0,), (0,)), ((), ())), preferred_element_type=F32)


def turn(x, cosine, sine):
    return x * cosine + pltpu.roll(x, 64, 1) * sine


def turn_back(x, cosine, sine):
    return x * cosine - pltpu.roll(x, 64, 1) * sine


def cols(n, width=HEAD_DIM):
    return slice(n * width, (n + 1) * width)


def attend(keys, values, queries, cotan, logsum, delta, mask=None):
    p = jnp.exp(nt(keys, queries) * FACTOR - logsum)
    if mask is not None:
        p = p * mask
    dv = nn(p.astype(BF), cotan)
    dp = nt(values, cotan)
    ds = (p * (dp - delta) * FACTOR).astype(BF)
    return tn(ds, keys), nn(ds, queries), dv


def kernel(
    off_ref, cnt_ref, sq, so, sg, sl, ik, iv, tq, tk, tv, to, tg, tl, cos_t, sin_t,
    sqg, ikg, ivg, tqg, tkg, tvg,
    qgs, dls, qgr, dlr, ks, kall, vall, qg, st, stp, tkr, tm, qtk, dqt, dkt, dvt, xt,
    dq, dk, dv, xk, dks, dvs, rss, rsr, sqs, sqr, tx,
    s_z, r_zqg, r_zd, r_zk, r_zv, s_xy, r_xyq, r_xys, s_sib, r_sib,
    s_o, r_ok, r_ov, r_oq, s_rs, r_rs, s_tx, r_tx,
):
    blk = lax.axis_index("blk")
    h = lax.axis_index("head")
    c = lax.rem(blk, 2)
    b = blk // 2
    lane = lax.broadcasted_iota(jnp.int32, (1, HEAD_DIM), 1)
    first = lax.rem(lane, 64) < 32
    sib = {"blk": 2 * b + 1 - c}

    def zdev(t):
        return lax.rem(h + t, NZ)

    def xydev(t):
        return lax.rem(b + t, NB)

    def remote(src, dst, ss, rs, dev):
        return pltpu.make_async_remote_copy(
            src_ref=src, dst_ref=dst, send_sem=ss, recv_sem=rs, device_id=dev, device_id_type=MESH
        )

    def angles(row, start, count):
        ct = cos_t[pl.ds(start, count), :]
        sn = sin_t[pl.ds(start, count), :]
        cr = cos_t[pl.ds(row, 1), :]
        sr = sin_t[pl.ds(row, 1), :]
        return jnp.where(first, cr, ct), jnp.where(first, sr, sn)

    place = off_ref[0] + blk
    row_at = lax.broadcasted_iota(jnp.int32, (32, 1), 0) == place // 4
    col_at = lax.rem(place, 4)

    def slab_angles(start, count):
        result = []
        for table in (cos_t, sin_t):
            row = jnp.sum(jnp.where(row_at, table[:32, :], 0.0), axis=0, keepdims=True)
            col = table[pl.ds(start, count), :]
            for i in range(1, 4):
                col = jnp.where(col_at == i, table[pl.ds(64 * i + start, count), :], col)
            result.append(jnp.where(first, row, col))
        return result

    bar = pltpu.get_barrier_semaphore()

    def greet_z(t, carry):
        pl.semaphore_signal(bar, inc=1, device_id={"head": zdev(t)}, device_id_type=MESH)
        return carry

    def greet_xy(t, carry):
        pl.semaphore_signal(bar, inc=1, device_id={"blk": 2 * xydev(t) + c}, device_id_type=MESH)
        return carry

    lax.fori_loop(1, NZ, greet_z, 0)
    lax.fori_loop(1, NB, greet_xy, 0)
    pl.semaphore_signal(bar, inc=1, device_id=sib, device_id_type=MESH)

    cq, sn_q = slab_angles(pl.multiple_of(8 * h, 8), 8)
    for d in range(NZ):
        acc = jnp.zeros((8, HEAD_DIM), F32)
        for j in range(HD):
            n = d * HD + j
            g = sg[:, cols(n)].astype(F32)
            q = turn(sq[:, cols(n)].astype(F32), cq, sn_q)
            qgs[:, cols(n)] = jnp.concatenate([q, g], axis=0).astype(BF)
            own = jnp.sum(g * so[:, cols(n)].astype(F32), axis=1, keepdims=True)
            acc = jnp.where(lane == j, own, acc)
        dls[d] = acc
    pl.semaphore_wait(bar, NZ + NB - 1)

    def wide(d):
        return pl.ds(pl.multiple_of(d * W, W), W)

    def z_qg(t, d):
        return remote(qgs.at[:, wide(d)], qgr.at[h], s_z.at[0, t], r_zqg.at[h], {"head": d})

    def z_dl(t, d):
        return remote(dls.at[d], dlr.at[h], s_z.at[1, t], r_zd.at[h], {"head": d})

    def key_rows(s):
        return pl.ds(pl.multiple_of(c * KEYS + s * 32, 32), 32)

    def z_k(t, d):
        return remote(ks.at[:, wide(d)], kall.at[key_rows(h), :], s_z.at[2, t], r_zk.at[h], {"head": d})

    def z_v(t, d):
        return remote(iv.at[:, wide(d)], vall.at[key_rows(h), :], s_z.at[3, t], r_zv.at[h], {"head": d})

    def go_qg(t, carry):
        z_qg(t, zdev(t)).start()
        z_dl(t, zdev(t)).start()
        return carry

    def go_v(t, carry):
        z_v(t, zdev(t)).start()
        return carry

    def go_k(t, carry):
        z_k(t, zdev(t)).start()
        return carry

    lax.fori_loop(1, NZ, go_qg, 0)
    lax.fori_loop(1, NZ, go_v, 0)
    ck, sn_k = angles(blk, pl.multiple_of(32 * h, 32), 32)
    for n in range(NZ * HD):
        ks[:, cols(n)] = turn(ik[:, cols(n)].astype(F32), ck, sn_k).astype(BF)
    lax.fori_loop(1, NZ, go_k, 0)
    kall[key_rows(h), :] = ks[:, wide(h)]
    vall[key_rows(h), :] = iv[:, wide(h)]
    qgr[h] = qgs[:, wide(h)]
    dlr[h] = dls[h]

    half = pl.ds(pl.multiple_of(HALF * c, HALF), HALF)
    ct = cos_t[pl.ds(pl.multiple_of(TXT + HALF * c, HALF), HALF), :]
    sn = sin_t[pl.ds(pl.multiple_of(TXT + HALF * c, HALF), HALF), :]
    acc = jnp.zeros((HALF, HEAD_DIM), F32)
    for j in range(HD):
        g = tg[half, cols(j)]
        qg[0, SLAB_Q:, cols(j)] = turn(tq[half, cols(j)].astype(F32), ct, sn).astype(BF)
        qg[1, SLAB_Q:, cols(j)] = g
        own = jnp.sum(g.astype(F32) * to[half, cols(j)].astype(F32), axis=1, keepdims=True)
        acc = jnp.where(lane == j, own, acc)
        acc = jnp.where(lane == HD + j, tl[half, j : j + 1], acc)
        tkr[:, cols(j)] = turn(tk[:, cols(j)].astype(F32), cos_t[TXT:, :], sin_t[TXT:, :]).astype(BF)
    tm[...] = acc
    stp[:, SLAB_Q:] = acc.T[:8, :]

    def wait_qg(t, carry):
        s = zdev(t)
        remote(qgs.at[:, wide(s)], qgr.at[s], s_z.at[0, t], r_zqg.at[s], {"head": s}).wait_recv()
        remote(dls.at[s], dlr.at[s], s_z.at[1, t], r_zd.at[s], {"head": s}).wait_recv()
        return carry

    lax.fori_loop(1, NZ, wait_qg, 0)
    both = qgr[...].astype(F32)
    own_q = both[:, :8, :].reshape(ROWS, W).astype(BF)
    own_g = both[:, 8:, :].reshape(ROWS, W).astype(BF)
    my_rows = pl.ds(pl.multiple_of(ROWS * b, ROWS), ROWS)
    qg[0, my_rows, :] = own_q
    qg[1, my_rows, :] = own_g
    stats = dlr[...].reshape(ROWS, HEAD_DIM)
    for j in range(HD):
        stats = jnp.where(lane == HD + j, sl[:, j : j + 1], stats)
    odd = lax.rem(b, 2) == 1
    blank = jnp.zeros_like(stats)
    spread = jnp.concatenate([jnp.where(odd, blank, stats), jnp.where(odd, stats, blank)], axis=0)
    st[b] = spread.T[:8, :]

    def xy_qg(t, e):
        return remote(
            qg.at[:, my_rows, :], qg.at[:, my_rows, :], s_xy.at[0, t], r_xyq.at[b], {"blk": 2 * e + c}
        )

    def xy_st(t, e):
        return remote(st.at[b], st.at[b], s_xy.at[1, t], r_xys.at[b], {"blk": 2 * e + c})

    def go_xy(t, carry):
        xy_qg(t, xydev(t)).start()
        xy_st(t, xydev(t)).start()
        return carry

    lax.fori_loop(1, NB, go_xy, 0)

    pair = pl.multiple_of(16 * (b // 2), 16)
    qtk[0, :ROWS, :] = own_q
    qtk[1, :ROWS, :] = own_g
    for i in range(2):
        qtk[i, ROWS : ROWS + 16, :] = qg[i, pl.ds(SLAB_Q + pair, 16), :]
        qtk[i, ROWS + 16 :, :] = jnp.zeros((HEAD_DIM - ROWS - 16, W), BF)
    index = lax.broadcasted_iota(jnp.int32, (16, 1), 0) // 8
    is_l = jnp.logical_and(lane >= HD, lane < 2 * HD)
    text_stats = jnp.where(
        jnp.logical_and(index != lax.rem(b, 2), is_l), SILENT, tm[pl.ds(pair, 16), :]
    )
    rest = jnp.broadcast_to(jnp.where(is_l, SILENT, 0.0), (HEAD_DIM - ROWS - 16, HEAD_DIM))
    tstats = jnp.concatenate([stats, text_stats, rest], axis=0).T
    key_index = lax.broadcasted_iota(jnp.int32, (TXT, 1), 0)
    mask = (key_index < cnt_ref[0]).astype(F32)
    for j in range(HD):
        one_q, one_k, one_v = attend(
            tkr[:, cols(j)], tv[:, cols(j)], qtk[0, :, cols(j)], qtk[1, :, cols(j)],
            tstats[HD + j : HD + j + 1, :], tstats[j : j + 1, :], mask,
        )
        dqt[:, cols(j)] = one_q
        dkt[:, cols(j)] = one_k
        dvt[:, cols(j)] = one_v
    other = pl.ds(pl.multiple_of(HALF * (1 - c), HALF), HALF)
    sib_tk = remote(dkt.at[other, :], xt.at[0], s_sib.at[0], r_sib.at[0], sib)
    sib_tv = remote(dvt.at[other, :], xt.at[1], s_sib.at[1], r_sib.at[1], sib)
    sib_tk.start()
    sib_tv.start()

    def wait_kv(t, carry):
        s = zdev(t)
        remote(iv.at[:, wide(s)], vall.at[key_rows(s), :], s_z.at[3, t], r_zv.at[s], {"head": s}).wait_recv()
        remote(ks.at[:, wide(s)], kall.at[key_rows(s), :], s_z.at[2, t], r_zk.at[s], {"head": s}).wait_recv()
        return carry

    lax.fori_loop(1, NZ, wait_kv, 0)
    mine = pl.ds(pl.multiple_of(KEYS * c, KEYS), KEYS)
    theirs = pl.ds(pl.multiple_of(KEYS * (1 - c), KEYS), KEYS)
    sib_k = remote(kall.at[mine, :], kall.at[mine, :], s_sib.at[2], r_sib.at[2], sib)
    sib_v = remote(vall.at[mine, :], vall.at[mine, :], s_sib.at[3], r_sib.at[3], sib)
    sib_k.start()
    sib_v.start()

    def wait_xy(t, carry):
        s = xydev(t)
        rows = pl.ds(pl.multiple_of(ROWS * s, ROWS), ROWS)
        remote(qg.at[:, rows, :], qg.at[:, rows, :], s_xy.at[0, t], r_xyq.at[s], {"blk": 2 * s + c}).wait_recv()
        remote(st.at[s], st.at[s], s_xy.at[1, t], r_xys.at[s], {"blk": 2 * s + c}).wait_recv()
        return carry

    lax.fori_loop(1, NB, wait_xy, 0)
    for i in range(NB // 2):
        stp[:, cols(i)] = st[2 * i] + st[2 * i + 1]
    remote(kall.at[theirs, :], kall.at[theirs, :], s_sib.at[2], r_sib.at[2], sib).wait_recv()
    remote(vall.at[theirs, :], vall.at[theirs, :], s_sib.at[3], r_sib.at[3], sib).wait_recv()

    for j in range(HD):
        keys = kall[:, cols(j)]
        values = vall[:, cols(j)]
        one_q, one_k, one_v = attend(
            keys, values, qg[0, SLAB_Q:, cols(j)], qg[1, SLAB_Q:, cols(j)],
            stp[HD + j : HD + j + 1, SLAB_Q:], stp[j : j + 1, SLAB_Q:],
        )
        dq[SLAB_Q:, cols(j)] = one_q
        dk[:, cols(j)] = one_k
        dv[:, cols(j)] = one_v

        def chunk(i, carry, j=j):
            rows = pl.ds(pl.multiple_of(i * 256, 256), 256)
            one_q, one_k, one_v = attend(
                kall[:, cols(j)], vall[:, cols(j)], qg[0, rows, cols(j)], qg[1, rows, cols(j)],
                stp[HD + j : HD + j + 1, rows], stp[j : j + 1, rows],
            )
            dq[rows, cols(j)] = one_q
            dk[:, cols(j)] += one_k
            dv[:, cols(j)] += one_v
            return carry

        lax.fori_loop(0, SLAB_Q // 256, chunk, 0)

    sib_dk = remote(dk.at[theirs, :], xk.at[0], s_sib.at[4], r_sib.at[4], sib)
    sib_dv = remote(dv.at[theirs, :], xk.at[1], s_sib.at[5], r_sib.at[5], sib)
    sib_dk.start()
    sib_dv.start()

    sib_tk.wait()
    sib_tv.wait()
    text_terms = [
        dq[SLAB_Q:, :].reshape(NB, 8, W),
        (dkt[half, :] + xt[0]).reshape(NB, 8, W),
        (dvt[half, :] + xt[1]).reshape(NB, 8, W),
        jnp.zeros((NB, 8, W), F32),
    ]
    rss[:, ROWS:, :] = jnp.concatenate(text_terms, axis=1).astype(BF)
    rss[:, :ROWS, :] = dq[:SLAB_Q, :].reshape(NB, ROWS, W).astype(BF)
    rsr[b] = rss[b]

    def rs(t, e):
        return remote(rss.at[e], rsr.at[b], s_rs.at[t], r_rs.at[b], {"blk": 2 * e + c})

    def go_rs(t, carry):
        rs(t, xydev(t)).start()
        return carry

    lax.fori_loop(1, NB, go_rs, 0)

    sib_dv.wait()
    sib_dk.wait()
    dvs[...] = (dv[mine, :] + xk[1]).astype(BF)
    ck, sn_k = angles(blk, 0, KEYS)
    for j in range(HD):
        dks[:, cols(j)] = turn_back(dk[mine, cols(j)] + xk[0, :, cols(j)], ck, sn_k).astype(BF)

    def token_rows(s):
        return pl.ds(pl.multiple_of(s * 32, 32), 32)

    def out_k(t, d):
        return remote(dks.at[token_rows(d), :], ikg.at[:, wide(h)], s_o.at[0, t], r_ok.at[h], {"head": d})

    def out_v(t, d):
        return remote(dvs.at[token_rows(d), :], ivg.at[:, wide(h)], s_o.at[1, t], r_ov.at[h], {"head": d})

    def go_out(t, carry):
        out_k(t, zdev(t)).start()
        out_v(t, zdev(t)).start()
        return carry

    lax.fori_loop(1, NZ, go_out, 0)
    ikg[:, wide(h)] = dks[token_rows(h), :]
    ivg[:, wide(h)] = dvs[token_rows(h), :]

    def wait_rs(t, carry):
        s = xydev(t)
        remote(rss.at[s], rsr.at[s], s_rs.at[t], r_rs.at[s], {"blk": 2 * s + c}).wait_recv()
        return carry

    lax.fori_loop(1, NB, wait_rs, 0)
    total = rsr[0].astype(F32)
    for i in range(1, NB):
        total = total + rsr[i].astype(F32)
    slab_total = total[:ROWS, :] + dqt[:ROWS, :]
    extra = jnp.where(odd, dqt[ROWS + 8 : ROWS + 16, :], dqt[ROWS : ROWS + 8, :])
    text_q = total[ROWS : ROWS + 8, :] + extra
    text_k = total[ROWS + 8 : ROWS + 16, :]
    text_v = total[ROWS + 16 : ROWS + 24, :]
    cq, sn_q = slab_angles(0, ROWS)
    text_at = pl.ds(pl.multiple_of(TXT + HALF * c + 8 * b, 8), 8)
    ct = cos_t[text_at, :]
    sn = sin_t[text_at, :]
    slab_parts = []
    text_parts = []
    for j in range(HD):
        slab_parts.append(turn_back(slab_total[:, cols(j)], cq, sn_q).reshape(NZ, 8, HEAD_DIM))
        text_parts.append(
            jnp.concatenate(
                [
                    turn_back(text_q[:, cols(j)], ct, sn),
                    turn_back(text_k[:, cols(j)], ct, sn),
                    text_v[:, cols(j)],
                    jnp.zeros((8, HEAD_DIM), F32),
                ],
                axis=0,
            )
        )
    for j in range(HD):
        tx[c, b, :, cols(j)] = text_parts[j].astype(BF)

    def tx_copy(t, e):
        return remote(tx.at[c, b], tx.at[c, b], s_tx.at[t], r_tx.at[b], {"blk": 2 * e + c})

    def go_tx(t, carry):
        tx_copy(t, xydev(t)).start()
        return carry

    lax.fori_loop(1, NB, go_tx, 0)
    low = jnp.concatenate([slab_parts[0], slab_parts[2]], axis=1).astype(BF)
    high = jnp.concatenate([slab_parts[1], jnp.zeros((NZ, 8, HEAD_DIM), F32)], axis=1).astype(BF)
    sqs[:, :, :HEAD_DIM] = low
    sqs[:, :, HEAD_DIM:] = high

    def out_q(t, d):
        return remote(sqs.at[d], sqr.at[h], s_o.at[2, t], r_oq.at[h], {"head": d})

    def go_oq(t, carry):
        out_q(t, zdev(t)).start()
        return carry

    lax.fori_loop(1, NZ, go_oq, 0)
    sqr[h] = sqs[h]

    def wait_tx(t, carry):
        s = xydev(t)
        remote(tx.at[c, s], tx.at[c, s], s_tx.at[t], r_tx.at[s], {"blk": 2 * s + c}).wait_recv()
        return carry

    lax.fori_loop(1, NB, wait_tx, 0)
    sib_tx = remote(tx.at[c], tx.at[c], s_sib.at[6], r_sib.at[6], sib)
    sib_tx.start()

    def wait_oq(t, carry):
        s = zdev(t)
        remote(sqs.at[s], sqr.at[s], s_o.at[2, t], r_oq.at[s], {"head": s}).wait_recv()
        return carry

    lax.fori_loop(1, NZ, wait_oq, 0)
    for s in range(NZ):
        piece = sqr[s].astype(F32)
        sqg[:, s * W : s * W + 128] = piece[:8, :128].astype(BF)
        sqg[:, s * W + 128 : s * W + 256] = piece[:8, 128:].astype(BF)
        sqg[:, s * W + 256 : s * W + 384] = piece[8:, :128].astype(BF)

    def wait_out(t, carry):
        s = zdev(t)
        remote(dks.at[token_rows(s), :], ikg.at[:, wide(s)], s_o.at[0, t], r_ok.at[s], {"head": s}).wait_recv()
        remote(dvs.at[token_rows(s), :], ivg.at[:, wide(s)], s_o.at[1, t], r_ov.at[s], {"head": s}).wait_recv()
        return carry

    lax.fori_loop(1, NZ, wait_out, 0)
    remote(tx.at[1 - c], tx.at[1 - c], s_sib.at[6], r_sib.at[6], sib).wait_recv()
    for core in range(2):
        block = tx[core].astype(F32)
        rows = slice(core * HALF, (core + 1) * HALF)
        tqg[rows, :] = block[:, :8, :].reshape(HALF, W).astype(BF)
        tkg[rows, :] = block[:, 8:16, :].reshape(HALF, W).astype(BF)
        tvg[rows, :] = block[:, 16:24, :].reshape(HALF, W).astype(BF)

    def drain_z(t, carry):
        d = zdev(t)
        z_qg(t, d).wait_send()
        z_dl(t, d).wait_send()
        z_k(t, d).wait_send()
        z_v(t, d).wait_send()
        out_k(t, d).wait_send()
        out_v(t, d).wait_send()
        out_q(t, d).wait_send()
        return carry

    def drain_xy(t, carry):
        e = xydev(t)
        xy_qg(t, e).wait_send()
        xy_st(t, e).wait_send()
        rs(t, e).wait_send()
        tx_copy(t, e).wait_send()
        return carry

    lax.fori_loop(1, NZ, drain_z, 0)
    lax.fori_loop(1, NB, drain_xy, 0)
    sib_k.wait_send()
    sib_v.wait_send()
    sib_tx.wait_send()


def on_device(
    slab_query, slab_output, slab_cotangent, slab_logsum, image_keys, image_values,
    text_query, text_keys, text_values, text_output, text_cotangent, text_logsum,
    text_count, slab_offsets,
):
    cos_t, sin_t = tables()
    vmem = pl.BlockSpec(memory_space=pltpu.VMEM)
    smem = pl.BlockSpec(memory_space=pltpu.SMEM)
    dma = pltpu.SemaphoreType.DMA
    shapes = [
        jax.ShapeDtypeStruct(x.shape, BF)
        for x in (slab_query, image_keys, image_values, text_query, text_keys, text_values)
    ]
    return pl.pallas_call(
        kernel,
        out_shape=shapes,
        in_specs=[smem, smem] + [vmem] * 14,
        out_specs=[vmem] * 6,
        scratch_shapes=[
            pltpu.VMEM((16, NZ * W), BF),
            pltpu.VMEM((NZ, 8, HEAD_DIM), F32),
            pltpu.VMEM((NZ, 16, W), BF),
            pltpu.VMEM((NZ, 8, HEAD_DIM), F32),
            pltpu.VMEM((32, NZ * W), BF),
            pltpu.VMEM((2 * KEYS, W), BF),
            pltpu.VMEM((2 * KEYS, W), BF),
            pltpu.VMEM((2, SLAB_Q + HALF, W), BF),
            pltpu.VMEM((NB, 8, HEAD_DIM), F32),
            pltpu.VMEM((8, SLAB_Q + HALF), F32),
            pltpu.VMEM((TXT, W), BF),
            pltpu.VMEM((HALF, HEAD_DIM), F32),
            pltpu.VMEM((2, HEAD_DIM, W), BF),
            pltpu.VMEM((HEAD_DIM, W), F32),
            pltpu.VMEM((TXT, W), F32),
            pltpu.VMEM((TXT, W), F32),
            pltpu.VMEM((2, HALF, W), F32),
            pltpu.VMEM((SLAB_Q + HALF, W), F32),
            pltpu.VMEM((2 * KEYS, W), F32),
            pltpu.VMEM((2 * KEYS, W), F32),
            pltpu.VMEM((2, KEYS, W), F32),
            pltpu.VMEM((KEYS, W), BF),
            pltpu.VMEM((KEYS, W), BF),
            pltpu.VMEM((NB, 96, W), BF),
            pltpu.VMEM((NB, 96, W), BF),
            pltpu.VMEM((NZ, 16, 256), BF),
            pltpu.VMEM((NZ, 16, 256), BF),
            pltpu.VMEM((2, NB, 32, W), BF),
            dma((4, NZ)), dma((NZ,)), dma((NZ,)), dma((NZ,)), dma((NZ,)),
            dma((2, NB)), dma((NB,)), dma((NB,)),
            dma((7,)), dma((7,)),
            dma((3, NZ)), dma((NZ,)), dma((NZ,)), dma((NZ,)),
            dma((NB,)), dma((NB,)), dma((NB,)), dma((NB,)),
        ],
        compiler_params=pltpu.CompilerParams(
            collective_id=0, has_side_effects=True, vmem_limit_bytes=48 * 1024 * 1024
        ),
        cost_estimate=pl.CostEstimate(
            flops=2_500_000_000, bytes_accessed=4_000_000, transcendentals=2_000_000
        ),
        name="joint_backward",
    )(
        slab_offsets, text_count, slab_query, slab_output, slab_cotangent, slab_logsum,
        image_keys, image_values, text_query, text_keys, text_values, text_output,
        text_cotangent, text_logsum, cos_t, sin_t,
    )


def solution(mesh):
    tokens = P(("rep", "blk", "head"), None)
    text = P("rep", "head")
    in_specs = (
        tokens, tokens, tokens, P(("rep", "blk"), "head"), tokens, tokens,
        text, text, text, text, text, text, P("rep"), P("rep"),
    )
    out_specs = (tokens, tokens, tokens, text, text, text)
    return jax.shard_map(
        on_device, mesh=mesh, in_specs=in_specs, out_specs=out_specs, check_vma=False
    )
```

time: 827 us -> 97.7 us (0.12)
  starting transfers between devices: 525 us -> 0 us
  waiting for transfers between devices: 202 us -> 0 us
  Pallas kernels: 0 us -> 81.8 us
  matrix products: 39.6 us -> 0 us
  between operations: 16 us -> 2.03 us
  other arithmetic: 12.7 us -> 0 us
    ppermute x160 -> x0, starting transfers between devices: 472 us -> none  [from_behind(): return lax.ppermute(value, axis, pairs)]
    psum x1 -> x0, waiting for transfers between devices: 130 us -> none  [on_device(): lax.psum((text_query_part, text_key_part, text_value_part), 'blk')]
    pallas_call x0 -> x1, Pallas kernels: none -> 81.8 us  [on_device(): pl.pallas_call(kernel, out_shape=shapes, in_specs=[smem, smem] + [vmem] *...]
    all_to_all x8 -> x0, starting transfers between devices: 52.7 us -> none  [the longest x1 13.1 us: on_device(): lax.all_to_all(slab_query, 'head', split_axis=1, concat_axis=0, tiled=True)]
    all_to_all x8 -> x0, waiting for transfers between devices: 47.7 us -> none  [the longest x1 9.69 us: on_device(): lax.all_to_all(image_values, 'head', split_axis=1, concat_axis=0, tiled=T...]
    dot_general x175 -> x0, matrix products: 39.6 us -> none  [the longest x35 10.6 us: attend(): jnp.einsum('hrn,rhd->nhd', score_grad, query_heads, preferred_element_typ...]
    ppermute x160 -> x0, waiting for transfers between devices: 23.6 us -> none  [from_behind(): return lax.ppermute(value, axis, pairs)]
  transfers between devices with their start and end apart: 169 -> 0, of which waited for: 23 -> 0; matrix products, arithmetic and copies ran while one was open for 8% -> 0% of each run, Pallas kernels for 0% -> 0%
where the time goes in v1:
time: 97.7 us; the launch traced here: 97.1 us
  Pallas kernels  81.8 us (84%)
  local copies, waits for them, and re-layouts  13.3 us (14%)
  between operations  2.03 us (2%)
    pallas_call x1, Pallas kernels, on_device(): pl.pallas_call(kernel, out_shape=shapes, in_specs=[smem, smem] + [vmem] *...  81.8 us
    unnamed x36, local copies, waits for them, and re-layouts  13.3 us

profile of v1, /device:TPU:1, one launch (start us, length us, event | category | flops | bytes accessed | tf_op | source)
XLA Modules:
  0.0 97.1 jit_solution(17137934150076651446)
XLA Ops:
  0.6 0.0 copy-start.13
  1.3 0.0 copy-start.12
  2.0 0.0 copy-done.13
  2.0 0.0 copy-start.9
  2.0 0.1 copy.22.sl
  2.1 0.0 copy-done.12
  2.1 0.0 copy-start.7
  2.1 0.0 copy-start.8
  2.1 0.1 copy.23.tl
  2.3 0.5 copy-done.9
  2.8 0.1 copy-done.7
  2.9 0.0 copy-done.8
  2.9 0.0 copy-start
  2.9 0.9 copy-done
  3.8 0.0 copy-start.1
  3.9 0.9 copy-done.1
  4.8 0.0 copy-start.2
  4.8 0.9 copy-done.2
  5.7 0.0 copy-start.3
  5.7 0.9 copy-done.3
  6.6 0.0 copy-start.4
  6.6 0.9 copy-done.4
  7.6 0.0 copy-start.5
  7.6 0.9 copy-done.5
  8.5 0.0 copy-start.6
  8.5 0.9 copy-done.6
  9.4 0.0 copy-start.10
  9.4 0.9 copy-done.10
  10.4 0.0 copy-start.11
  10.4 0.9 copy-done.11
  11.3 81.8 %joint_backward.1 = (bf16[8,3072]{1,0:T(8,128)(2,1)S(1)}, bf16[32,3072]{1,0:T(8,128)(2,1)S(1)}, bf16[32,3072]{1,0:T(8,128)(2,1)S(1)}, bf16[256,384]{1,0:T(8,128)...) custom-call(s32[1]{0:T(128)S(6)} %copy.31.off_ref, s32[1]{0:T(128)S(6)} %copy.30.cnt_ref, ...), custom_call_target="tpu_custom_call" | custom-call | flops 2500000000 | bytes 4000000 | tf_op jit(solution)/shard_map/joint_backward/pallas_call | solution.py:503
  93.1 0.6 copy.32
  93.7 0.7 copy.33
  94.4 0.7 copy.34
  95.1 0.7 copy.35
  95.7 0.7 copy.36
  96.4 0.7 copy.37
Async XLA Ops:
  0.6 1.3 %copy-start.13 = (f32[64,3]{0,1:T(4,128)S(1)}, f32[64,3]{0,1:T(4,128)}, u32[]{:S(2)}) copy-start(f32[64,3]{0,1:T(4,128)} %param.19) | copy-start | bytes 2308
  1.3 0.8 copy-start.12
  2.0 0.8 copy-start.9
  2.1 0.8 copy-start.7
  2.1 0.8 copy-start.8
  2.9 0.9 copy-start
  3.8 0.9 copy-start.1
  4.8 0.9 copy-start.2
  5.7 0.9 copy-start.3
  6.6 0.9 copy-start.4
  7.6 0.9 copy-start.5
  8.5 0.9 copy-start.6
  9.4 0.9 copy-start.10
  10.4 0.9 copy-start.11

commit v2 on v1

v2 whole, which is shorter than its diff:
```python
import jax
import jax.numpy as jnp
import numpy as np
from jax import lax
from jax.experimental import pallas as pl
from jax.experimental.pallas import tpu as pltpu
from jax.sharding import PartitionSpec as P

HEAD_DIM = 128
FACTOR = HEAD_DIM ** (-0.5)
NZ = 8
NX = 4
NB = NX * NX
HD = 3
W = HD * HEAD_DIM
ALL = NZ * W
TXT = 256
HALF = TXT // 2
ROWS = 64
KEYS = 256
SLAB_Q = NB * ROWS
STEP = 256
SILENT = 1e30
BF = jnp.bfloat16
F32 = jnp.float32
MESH = pl.DeviceIdType.MESH

TREE = (
    ((1, 0), (0, 0)),
    ((-1, 0), (0, 0)),
    ((0, 1), (0, 0)),
    ((0, -1), (0, 0)),
    ((1, 1), (1, 0)),
    ((-1, -1), (-1, 0)),
    ((1, -1), (0, -1)),
    ((-1, 1), (0, 1)),
    ((2, 0), (-1, 0)),
    ((0, 2), (0, -1)),
    ((2, 1), (1, 1)),
    ((2, -1), (1, -1)),
    ((1, 2), (1, 1)),
    ((-1, 2), (-1, 1)),
    ((2, 2), (-1, 2)),
)
NODE = [child for child, _ in TREE]
BELOW = {p: [k for k, (_, q) in enumerate(TREE) if q == p] for p in [(0, 0)] + NODE}
LEVELS = ((0, 1, 2, 3), (4, 5, 6, 7, 8, 9), (10, 11, 12, 13), (14,))
LEAVES = (14, 10, 12, 11, 8, 9, 5)
INNER = (13, 4, 6, 7, 0, 1, 2, 3)


def one_hop(step):
    return -1 if step in (-1, 3) else (1 if step in (1, -3) else 0 if step == 0 else -1)


def edge(k):
    (cx, cy), (px, py) = TREE[k]
    return one_hop(cx - px), one_hop(cy - py)


def tables():
    place = np.arange(512, dtype=np.float64)[:, None]
    frequency = 10000.0 ** (-np.arange(32, dtype=np.float64) / 32)
    angles = np.tile(place * frequency[None, :], (1, 4))
    sign = np.where(np.arange(128) < 64, -1.0, 1.0)
    return np.stack([np.cos(angles), np.sin(angles) * sign]).astype(np.float32)


def nt(a, b):
    return lax.dot_general(a, b, (((1,), (1,)), ((), ())), preferred_element_type=F32)


def nn(a, b):
    return lax.dot_general(a, b, (((1,), (0,)), ((), ())), preferred_element_type=F32)


def turn(x, cosine, sine):
    return x * cosine + pltpu.roll(x, 64, 1) * sine


def turn_back(x, cosine, sine):
    return x * cosine - pltpu.roll(x, 64, 1) * sine


def cols(n):
    return slice(n * HEAD_DIM, (n + 1) * HEAD_DIM)


def attend(keys, keys_t, values, queries, cotan, logsum, delta, mask=None):
    p = jnp.exp(nt(keys, queries) * FACTOR - logsum)
    if mask is not None:
        p = p * mask
    dv = nn(p.astype(BF), cotan)
    dp = nt(values, cotan)
    ds = (p * (dp - delta) * FACTOR).astype(BF)
    return nn(keys_t, ds).T, nn(ds, queries), dv


def kernel(
    off_ref, cnt_ref, sq_h, so_h, sg_h, sl_h, ik_h, iv_h, tq_h, tk_h, tv_h, to_h, tg_h, tl_h, tab_h,
    sqo, okv, txo,
    sq, so, sg, sl, ik, tq, tk, tv, to, tg, tl, tab,
    qgs, dls, qgr, dlr, kvs, kv, qg, st, stp, tkr, tst, qtk, dqt, dkvt, xt,
    dq, dkv, xk, dkvs, ts_s, ts_r, rs_s, rs_r, sqs, sqr, tx,
    s_in, s_z, r_zqg, r_zd, s_kv, r_kv, s_xy, r_xy, s_sib, r_sib, s_skv, r_skv, s_sd, r_sd,
    s_o, r_o, s_oq, r_oq, s_ts, r_ts, s_rs, r_rs, s_tx, r_tx,
):
    blk = lax.axis_index("blk")
    h = lax.axis_index("head")
    c = lax.rem(blk, 2)
    b = blk // 2
    bx = b // NX
    by = lax.rem(b, NX)
    lane = lax.broadcasted_iota(jnp.int32, (1, HEAD_DIM), 1)
    first = lax.rem(lane, 64) < 32
    sib = {"blk": 2 * b + 1 - c}

    def zdev(t):
        return lax.rem(h + t, NZ)

    def chip(dx, dy):
        return lax.rem(bx + dx + NX, NX) * NX + lax.rem(by + dy + NX, NX)

    def on_chip(e):
        return {"blk": 2 * e + c}

    def remote(src, dst, ss, rs, dev):
        return pltpu.make_async_remote_copy(
            src_ref=src, dst_ref=dst, send_sem=ss, recv_sem=rs, device_id=dev, device_id_type=MESH
        )

    def rows_of(e, count):
        return pl.ds(pl.multiple_of(e * count, count), count)

    def wide(d):
        return rows_of(d, W)

    def head_cols(d, j):
        return pl.ds(pl.multiple_of(d * W + j * HEAD_DIM, HEAD_DIM), HEAD_DIM)

    def fetch(i, src, dst):
        copy = pltpu.make_async_copy(src, dst, s_in.at[i])
        copy.start()
        return copy

    f_tab = fetch(0, tab_h, tab)
    f_slab = [fetch(1, sq_h, sq), fetch(2, sg_h, sg), fetch(3, so_h, so)]
    f_k = fetch(4, ik_h, ik)
    f_v = fetch(5, iv_h, kvs.at[1])
    f_text = [
        fetch(6, tq_h, tq), fetch(7, tg_h, tg), fetch(8, to_h, to), fetch(9, tk_h, tk),
        fetch(10, tv_h, tv), fetch(11, tl_h, tl), fetch(12, sl_h, sl),
    ]

    bar = pltpu.get_barrier_semaphore()

    def greet_z(t, carry):
        pl.semaphore_signal(bar, inc=1, device_id={"head": zdev(t)}, device_id_type=MESH)
        return carry

    lax.fori_loop(1, NZ, greet_z, 0)
    for dx, dy in ((1, 0), (-1, 0), (0, 1), (0, -1)):
        pl.semaphore_signal(bar, inc=1, device_id=on_chip(chip(dx, dy)), device_id_type=MESH)
    pl.semaphore_signal(bar, inc=1, device_id=sib, device_id_type=MESH)

    cos_t, sin_t = tab.at[0], tab.at[1]

    def angles(row, start, count):
        ct = cos_t[pl.ds(start, count), :]
        sn = sin_t[pl.ds(start, count), :]
        cr = cos_t[pl.ds(row, 1), :]
        sr = sin_t[pl.ds(row, 1), :]
        return jnp.where(first, cr, ct), jnp.where(first, sr, sn)

    place = off_ref[0] + blk
    row_at = lax.broadcasted_iota(jnp.int32, (32, 1), 0) == place // 4
    col_at = lax.rem(place, 4)

    def slab_angles(start, count):
        result = []
        for table in (cos_t, sin_t):
            row = jnp.sum(jnp.where(row_at, table[:32, :], 0.0), axis=0, keepdims=True)
            col = table[pl.ds(start, count), :]
            for i in range(1, 4):
                col = jnp.where(col_at == i, table[pl.ds(64 * i + start, count), :], col)
            result.append(jnp.where(first, row, col))
        return result

    f_tab.wait()
    for copy in f_slab:
        copy.wait()
    cq, sn_q = slab_angles(pl.multiple_of(8 * h, 8), 8)
    for d in range(NZ):
        acc = jnp.zeros((8, HEAD_DIM), F32)
        for j in range(HD):
            n = d * HD + j
            g = sg[:, cols(n)].astype(F32)
            q = turn(sq[:, cols(n)].astype(F32), cq, sn_q)
            qgs[:, cols(n)] = jnp.concatenate([q, g], axis=0).astype(BF)
            own = jnp.sum(g * so[:, cols(n)].astype(F32), axis=1, keepdims=True)
            acc = jnp.where(lane == j, own, acc)
        dls[d] = acc
    pl.semaphore_wait(bar, NZ + NX)

    def z_qg(t, d):
        return remote(qgs.at[:, wide(d)], qgr.at[h], s_z.at[0, t], r_zqg.at[h], {"head": d})

    def z_dl(t, d):
        return remote(dls.at[d], dlr.at[h], s_z.at[1, t], r_zd.at[h], {"head": d})

    def key_rows(s):
        return pl.ds(pl.multiple_of(c * KEYS + s * 32, 32), 32)

    def z_kv(j, t, d):
        return remote(
            kvs.at[:, :, head_cols(d, j)], kv.at[:, key_rows(h), cols(j)],
            s_kv.at[j, t], r_kv.at[j, h], {"head": d},
        )

    def go_qg(t, carry):
        z_qg(t, zdev(t)).start()
        z_dl(t, zdev(t)).start()
        return carry

    lax.fori_loop(1, NZ, go_qg, 0)
    f_k.wait()
    f_v.wait()
    ck, sn_k = angles(blk, pl.multiple_of(32 * h, 32), 32)
    for j in range(HD):
        for d in range(NZ):
            n = d * HD + j
            kvs[0, :, cols(n)] = turn(ik[:, cols(n)].astype(F32), ck, sn_k).astype(BF)

        def go_kv(t, carry, j=j):
            z_kv(j, t, zdev(t)).start()
            return carry

        lax.fori_loop(1, NZ, go_kv, 0)
    kv[:, key_rows(h), :] = kvs[:, :, wide(h)]
    qgr[h] = qgs[:, wide(h)]
    dlr[h] = dls[h]

    for copy in f_text:
        copy.wait()
    half = rows_of(c, HALF)
    text_at = pl.ds(pl.multiple_of(TXT + HALF * c, HALF), HALF)
    ct = cos_t[text_at, :]
    sn = sin_t[text_at, :]
    acc = jnp.zeros((HALF, HEAD_DIM), F32)
    for j in range(HD):
        g = tg[half, cols(j)]
        qg[0, SLAB_Q:, cols(j)] = turn(tq[half, cols(j)].astype(F32), ct, sn).astype(BF)
        qg[1, SLAB_Q:, cols(j)] = g
        own = jnp.sum(g.astype(F32) * to[half, cols(j)].astype(F32), axis=1, keepdims=True)
        acc = jnp.where(lane == j, own, acc)
        tkr[:, cols(j)] = turn(tk[:, cols(j)].astype(F32), cos_t[TXT:, :], sin_t[TXT:, :]).astype(BF)
    stp[:, SLAB_Q:] = acc.T[:8, :]
    stp[HD : 2 * HD, SLAB_Q:] = tl[:, half]

    def wait_qg(t, carry):
        s = zdev(t)
        remote(qgs.at[:, wide(s)], qgr.at[s], s_z.at[0, t], r_zqg.at[s], {"head": s}).wait_recv()
        remote(dls.at[s], dlr.at[s], s_z.at[1, t], r_zd.at[s], {"head": s}).wait_recv()
        return carry

    lax.fori_loop(1, NZ, wait_qg, 0)
    both = qgr[...].astype(F32)
    own_q = both[:, :8, :].reshape(ROWS, W).astype(BF)
    own_g = both[:, 8:, :].reshape(ROWS, W).astype(BF)
    my_rows = rows_of(b, ROWS)
    qg[0, my_rows, :] = own_q
    qg[1, my_rows, :] = own_g
    odd = lax.rem(b, 2) == 1
    delta = dlr[...].reshape(ROWS, HEAD_DIM)
    blank = jnp.zeros_like(delta)
    spread = jnp.concatenate([jnp.where(odd, blank, delta), jnp.where(odd, delta, blank)], axis=0)
    here = (lane // 64) == lax.rem(b, 2)
    logs = jnp.concatenate([sl[...], sl[...]], axis=1)
    st[b] = spread.T[:8, :]
    st[b, HD : 2 * HD, :] = jnp.where(here, logs, 0.0)

    def ag(k, s, e):
        return (
            remote(qg.at[:, rows_of(s, ROWS), :], qg.at[:, rows_of(s, ROWS), :], s_xy.at[0, k], r_xy.at[0, k], on_chip(e)),
            remote(st.at[s], st.at[s], s_xy.at[1, k], r_xy.at[1, k], on_chip(e)),
        )

    def ag_send(k):
        (_, _), (px, py) = TREE[k]
        dx, dy = edge(k)
        return ag(k, chip(-px, -py), chip(dx, dy))

    def ag_start(node):
        for k in BELOW[node]:
            for copy in ag_send(k):
                copy.start()

    def ag_level(level):
        for k in LEVELS[level]:
            cx, cy = NODE[k]
            for copy in ag(k, chip(-cx, -cy), b):
                copy.wait_recv()
            ag_start(NODE[k])

    ag_start((0, 0))

    pair = pl.multiple_of(16 * (b // 2), 16)
    qtk[0, :ROWS, :] = own_q
    qtk[1, :ROWS, :] = own_g
    for i in range(2):
        qtk[i, ROWS : ROWS + 16, :] = qg[i, pl.ds(SLAB_Q + pair, 16), :]
        qtk[i, ROWS + 16 :, :] = jnp.zeros((HEAD_DIM - ROWS - 16, W), BF)
    own_st = st[b]
    own_st = jnp.where(odd, pltpu.roll(own_st, 64, 1), own_st)
    text_st = pltpu.roll(stp[:, SLAB_Q:], lax.rem(ROWS - pair + HEAD_DIM, HEAD_DIM), 1)
    mine_at = lane // 8 == ROWS // 8 + lax.rem(b, 2)
    stat_row = lax.broadcasted_iota(jnp.int32, (8, 1), 0)
    silent = jnp.where(jnp.logical_and(stat_row >= HD, stat_row < 2 * HD), SILENT, 0.0)
    tst[...] = jnp.where(lane < ROWS, own_st, jnp.where(mine_at, text_st, silent))
    key_index = lax.broadcasted_iota(jnp.int32, (TXT, 1), 0)
    mask = (key_index < cnt_ref[0]).astype(F32)

    def text_keys(j):
        keys = tkr[:, cols(j)]
        one_q, one_k, one_v = attend(
            keys, keys.T, tv[:, cols(j)], qtk[0, :, cols(j)], qtk[1, :, cols(j)],
            tst[HD + j : HD + j + 1, :], tst[j : j + 1, :], mask,
        )
        dqt[:, cols(j)] = one_q
        dkvt[0, :, cols(j)] = one_k
        dkvt[1, :, cols(j)] = one_v

    text_keys(0)
    ag_level(0)
    text_keys(1)
    text_keys(2)
    other = rows_of(1 - c, HALF)
    sib_t = remote(dkvt.at[:, other, :], xt, s_sib.at[0], r_sib.at[0], sib)
    sib_t.start()
    ag_level(1)

    mine = rows_of(c, KEYS)
    theirs = rows_of(1 - c, KEYS)

    def sib_kv(j, rows):
        part = kv.at[:, rows, cols(j)]
        return remote(part, part, s_skv.at[j], r_skv.at[j], sib)

    def share_kv(j):
        def wait_kv(t, carry):
            s = zdev(t)
            remote(
                kvs.at[:, :, head_cols(s, j)], kv.at[:, key_rows(s), cols(j)],
                s_kv.at[j, t], r_kv.at[j, s], {"head": s},
            ).wait_recv()
            return carry

        lax.fori_loop(1, NZ, wait_kv, 0)
        sib_kv(j, mine).start()

    share_kv(0)
    ag_level(2)
    ag_level(3)
    for i in range(NB // 2):
        stp[:, cols(i)] = st[2 * i] + st[2 * i + 1]
    share_kv(1)

    def image_keys(j, keys_t, rows, start):
        one_q, one_k, one_v = attend(
            kv[0, :, cols(j)], keys_t, kv[1, :, cols(j)], qg[0, rows, cols(j)], qg[1, rows, cols(j)],
            stp[HD + j : HD + j + 1, rows], stp[j : j + 1, rows],
        )
        dq[rows, cols(j)] = one_q
        if start:
            dkv[0, :, cols(j)] = one_k
            dkv[1, :, cols(j)] = one_v
        else:
            dkv[0, :, cols(j)] += one_k
            dkv[1, :, cols(j)] += one_v

    def slab_queries(j, keys_t):
        for i in range(SLAB_Q // STEP):
            image_keys(j, keys_t, slice(i * STEP, (i + 1) * STEP), False)

    def sib_d(j):
        return remote(dkv.at[:, theirs, cols(j)], xk.at[:, :, cols(j)], s_sd.at[j], r_sd.at[j], sib)

    ck, sn_k = angles(blk, 0, KEYS)

    def token_rows(s):
        return rows_of(s, 32)

    def z_out(j, t, d):
        return remote(
            dkvs.at[:, token_rows(d), cols(j)], okv.at[:, :, head_cols(h, j)],
            s_o.at[j, t], r_o.at[j, h], {"head": d},
        )

    def finish_kv(j):
        sib_d(j).wait()
        dkvs[0, :, cols(j)] = turn_back(dkv[0, mine, cols(j)] + xk[0, :, cols(j)], ck, sn_k).astype(BF)
        dkvs[1, :, cols(j)] = (dkv[1, mine, cols(j)] + xk[1, :, cols(j)]).astype(BF)

        def go_out(t, carry):
            z_out(j, t, zdev(t)).start()
            return carry

        lax.fori_loop(1, NZ, go_out, 0)
        okv[:, :, head_cols(h, j)] = dkvs[:, token_rows(h), cols(j)]

    def make_sum(own, sent, got, ss, rs):
        def send(k):
            dx, dy = edge(k)
            return remote(sent.at[k], got.at[k], ss.at[k], rs.at[k], on_chip(chip(-dx, -dy)))

        def gather(node):
            value = own(chip(-node[0], -node[1]))
            for k in BELOW[node]:
                send(k).wait_recv()
                value = value + got[k].astype(F32)
            return value

        def pass_on(k):
            sent[k] = gather(NODE[k]).astype(BF)
            send(k).start()

        return send, gather, pass_on

    def own_text(e):
        at = rows_of(e, 8)
        at_half = pl.ds(pl.multiple_of(HALF * c + e * 8, 8), 8)
        return jnp.concatenate(
            [
                dq[pl.ds(pl.multiple_of(SLAB_Q + e * 8, 8), 8), :],
                dkvt[0, at_half, :] + xt[0, at, :],
                dkvt[1, at_half, :] + xt[1, at, :],
                jnp.zeros((8, W), F32),
            ],
            axis=0,
        )

    def own_slab(e):
        return dq[rows_of(e, ROWS), :]

    ts_send, ts_gather, ts_pass = make_sum(own_text, ts_s, ts_r, s_ts, r_ts)
    rs_send, rs_gather, rs_pass = make_sum(own_slab, rs_s, rs_r, s_rs, r_rs)

    for j in range(HD):
        sib_kv(j, theirs).wait_recv()
        keys_t = kv[0, :, cols(j)].T
        image_keys(j, keys_t, slice(SLAB_Q, SLAB_Q + HALF), True)
        if j == HD - 1:
            sib_t.wait()
            for k in LEAVES:
                ts_pass(k)
        slab_queries(j, keys_t)
        sib_d(j).start()
        if j == 0:
            share_kv(2)
        if j > 0:
            finish_kv(j - 1)
    for k in LEAVES:
        rs_pass(k)
    ts_pass(INNER[0])
    finish_kv(HD - 1)
    rs_pass(INNER[0])
    for k in INNER[1:]:
        ts_pass(k)
        rs_pass(k)

    total = ts_gather((0, 0))
    extra = jnp.where(odd, dqt[ROWS + 8 : ROWS + 16, :], dqt[ROWS : ROWS + 8, :])
    text_q = total[:8, :] + extra
    text_k = total[8:16, :]
    text_v = total[16:24, :]
    own_at = pl.ds(pl.multiple_of(TXT + HALF * c + 8 * b, 8), 8)
    ct = cos_t[own_at, :]
    sn = sin_t[own_at, :]
    for j in range(HD):
        tx[c, b, :, cols(j)] = jnp.concatenate(
            [
                turn_back(text_q[:, cols(j)], ct, sn),
                turn_back(text_k[:, cols(j)], ct, sn),
                text_v[:, cols(j)],
                jnp.zeros((8, HEAD_DIM), F32),
            ],
            axis=0,
        ).astype(BF)

    def tx_copy(k, s, e):
        return remote(tx.at[c, s], tx.at[c, s], s_tx.at[k], r_tx.at[k], on_chip(e))

    def tx_send(k):
        (_, _), (px, py) = TREE[k]
        dx, dy = edge(k)
        return tx_copy(k, chip(-px, -py), chip(dx, dy))

    def tx_start(node):
        for k in BELOW[node]:
            tx_send(k).start()

    def tx_level(level):
        for k in LEVELS[level]:
            cx, cy = NODE[k]
            tx_copy(k, chip(-cx, -cy), b).wait_recv()
            tx_start(NODE[k])

    tx_start((0, 0))
    slab_total = rs_gather((0, 0)) + dqt[:ROWS, :]
    cq, sn_q = slab_angles(0, ROWS)
    parts = [turn_back(slab_total[:, cols(j)], cq, sn_q).reshape(NZ, 8, HEAD_DIM) for j in range(HD)]
    sqs[:, :, :HEAD_DIM] = jnp.concatenate([parts[0], parts[2]], axis=1).astype(BF)
    sqs[:, :, HEAD_DIM:] = jnp.concatenate([parts[1], jnp.zeros_like(parts[1])], axis=1).astype(BF)

    def out_q(t, d):
        return remote(sqs.at[d], sqr.at[h], s_oq.at[t], r_oq.at[h], {"head": d})

    def go_oq(t, carry):
        out_q(t, zdev(t)).start()
        return carry

    lax.fori_loop(1, NZ, go_oq, 0)
    sqr[h] = sqs[h]
    for level in range(4):
        tx_level(level)
    sib_tx = remote(tx.at[c], tx.at[c], s_sib.at[1], r_sib.at[1], sib)
    sib_tx.start()

    def wait_oq(t, carry):
        s = zdev(t)
        remote(sqs.at[s], sqr.at[s], s_oq.at[t], r_oq.at[s], {"head": s}).wait_recv()
        return carry

    lax.fori_loop(1, NZ, wait_oq, 0)
    for s in range(NZ):
        piece = sqr[s].astype(F32)
        sqo[:, s * W : s * W + 128] = piece[:8, :128].astype(BF)
        sqo[:, s * W + 128 : s * W + 256] = piece[:8, 128:].astype(BF)
        sqo[:, s * W + 256 : s * W + 384] = piece[8:, :128].astype(BF)
    remote(tx.at[1 - c], tx.at[1 - c], s_sib.at[1], r_sib.at[1], sib).wait_recv()
    for core in range(2):
        block = tx[core].astype(F32)
        rows = slice(core * HALF, (core + 1) * HALF)
        for i in range(3):
            txo[i, rows, :] = block[:, 8 * i : 8 * i + 8, :].reshape(HALF, W).astype(BF)
    for j in range(HD):

        def wait_out(t, carry, j=j):
            s = zdev(t)
            remote(
                dkvs.at[:, token_rows(s), cols(j)], okv.at[:, :, head_cols(s, j)],
                s_o.at[j, t], r_o.at[j, s], {"head": s},
            ).wait_recv()
            return carry

        lax.fori_loop(1, NZ, wait_out, 0)

    def drain_z(t, carry):
        d = zdev(t)
        z_qg(t, d).wait_send()
        z_dl(t, d).wait_send()
        out_q(t, d).wait_send()
        for j in range(HD):
            z_kv(j, t, d).wait_send()
            z_out(j, t, d).wait_send()
        return carry

    lax.fori_loop(1, NZ, drain_z, 0)
    for k in range(len(TREE)):
        for copy in ag_send(k):
            copy.wait_send()
        ts_send(k).wait_send()
        rs_send(k).wait_send()
        tx_send(k).wait_send()
    for j in range(HD):
        sib_kv(j, mine).wait_send()
    sib_tx.wait_send()


def deliver(sqo, okv, txo, sqg, ikg, ivg, tqg, tkg, tvg, sems):
    pairs = (
        (sqo, sqg), (okv.at[0], ikg), (okv.at[1], ivg),
        (txo.at[0], tqg), (txo.at[1], tkg), (txo.at[2], tvg),
    )
    copies = [pltpu.make_async_copy(a, b, sems.at[i]) for i, (a, b) in enumerate(pairs)]
    for copy in copies:
        copy.start()
    for copy in copies:
        copy.wait()


def on_device(
    slab_query, slab_output, slab_cotangent, slab_logsum, image_keys, image_values,
    text_query, text_keys, text_values, text_output, text_cotangent, text_logsum,
    text_count, slab_offsets,
):
    vmem = pl.BlockSpec(memory_space=pltpu.VMEM)
    smem = pl.BlockSpec(memory_space=pltpu.SMEM)
    hbm = pl.BlockSpec(memory_space=pltpu.HBM)
    dma = pltpu.SemaphoreType.DMA
    edges = len(TREE)
    slab = pltpu.VMEM((8, ALL), BF)
    text = pltpu.VMEM((TXT, W), BF)
    sqo, okv, txo = pl.pallas_call(
        kernel,
        out_shape=[
            jax.ShapeDtypeStruct((8, ALL), BF),
            jax.ShapeDtypeStruct((2, 32, ALL), BF),
            jax.ShapeDtypeStruct((3, TXT, W), BF),
        ],
        in_specs=[smem, smem] + [hbm] * 13,
        out_specs=[vmem] * 3,
        scratch_shapes=[
            slab, slab, slab,
            pltpu.VMEM((HD, ROWS), F32),
            pltpu.VMEM((32, ALL), BF),
            text, text, text, text, text,
            pltpu.VMEM((HD, TXT), F32),
            pltpu.VMEM((2, 512, HEAD_DIM), F32),
            pltpu.VMEM((16, ALL), BF),
            pltpu.VMEM((NZ, 8, HEAD_DIM), F32),
            pltpu.VMEM((NZ, 16, W), BF),
            pltpu.VMEM((NZ, 8, HEAD_DIM), F32),
            pltpu.VMEM((2, 32, ALL), BF),
            pltpu.VMEM((2, 2 * KEYS, W), BF),
            pltpu.VMEM((2, SLAB_Q + HALF, W), BF),
            pltpu.VMEM((NB, 8, HEAD_DIM), F32),
            pltpu.VMEM((8, SLAB_Q + HALF), F32),
            pltpu.VMEM((TXT, W), BF),
            pltpu.VMEM((8, HEAD_DIM), F32),
            pltpu.VMEM((2, HEAD_DIM, W), BF),
            pltpu.VMEM((HEAD_DIM, W), F32),
            pltpu.VMEM((2, TXT, W), F32),
            pltpu.VMEM((2, HALF, W), F32),
            pltpu.VMEM((SLAB_Q + HALF, W), F32),
            pltpu.VMEM((2, 2 * KEYS, W), F32),
            pltpu.VMEM((2, KEYS, W), F32),
            pltpu.VMEM((2, KEYS, W), BF),
            pltpu.VMEM((edges, 32, W), BF),
            pltpu.VMEM((edges, 32, W), BF),
            pltpu.VMEM((edges, ROWS, W), BF),
            pltpu.VMEM((edges, ROWS, W), BF),
            pltpu.VMEM((NZ, 16, 256), BF),
            pltpu.VMEM((NZ, 16, 256), BF),
            pltpu.VMEM((2, NB, 32, W), BF),
            dma((13,)),
            dma((2, NZ)), dma((NZ,)), dma((NZ,)),
            dma((HD, NZ)), dma((HD, NZ)),
            dma((2, edges)), dma((2, edges)),
            dma((2,)), dma((2,)),
            dma((HD,)), dma((HD,)), dma((HD,)), dma((HD,)),
            dma((HD, NZ)), dma((HD, NZ)),
            dma((NZ,)), dma((NZ,)),
            dma((edges,)), dma((edges,)),
            dma((edges,)), dma((edges,)),
            dma((edges,)), dma((edges,)),
        ],
        compiler_params=pltpu.CompilerParams(
            collective_id=0, has_side_effects=True, vmem_limit_bytes=48 * 1024 * 1024
        ),
        cost_estimate=pl.CostEstimate(
            flops=2_500_000_000, bytes_accessed=4_000_000, transcendentals=2_000_000
        ),
        name="joint_backward",
    )(
        slab_offsets, text_count, slab_query, slab_output, slab_cotangent, slab_logsum.T,
        image_keys, image_values, text_query, text_keys, text_values, text_output,
        text_cotangent, text_logsum.T, tables(),
    )
    shapes = [
        jax.ShapeDtypeStruct(x.shape, BF)
        for x in (slab_query, image_keys, image_values, text_query, text_keys, text_values)
    ]
    anywhere = pl.BlockSpec(memory_space=pl.ANY)
    return pl.pallas_call(
        deliver,
        out_shape=shapes,
        in_specs=[anywhere] * 3,
        out_specs=[anywhere] * 6,
        scratch_shapes=[dma((6,))],
        name="deliver",
    )(sqo, okv, txo)


def solution(mesh):
    tokens = P(("rep", "blk", "head"), None)
    text = P("rep", "head")
    in_specs = (
        tokens, tokens, tokens, P(("rep", "blk"), "head"), tokens, tokens,
        text, text, text, text, text, text, P("rep"), P("rep"),
    )
    out_specs = (tokens, tokens, tokens, text, text, text)
    return jax.shard_map(
        on_device, mesh=mesh, in_specs=in_specs, out_specs=out_specs, check_vma=False
    )
```

time: 97.7 us -> 130 us (1.33)
  the two profiles are of different devices: /device:TPU:1 before, /device:TPU:131 now
where the time goes in v2:
time: 130 us
  Pallas kernels  115 us (88%)
  local copies, waits for them, and re-layouts  12.8 us (10%)
  between operations  2 us (2%)
    pallas_call x1, Pallas kernels, on_device(): pl.pallas_call(kernel, out_shape=[jax.ShapeDtypeStruct((8, ALL), BF), jax...  82.3 us
    pallas_call x1, Pallas kernels, on_device(): pl.pallas_call(deliver, out_shape=shapes, in_specs=[anywhere] * 3, out_sp...  32.4 us
    unnamed x32, local copies, waits for them, and re-layouts  12.8 us

profile of v2, /device:TPU:131, one launch (start us, length us, event | category | flops | bytes accessed | tf_op | source)
XLA Modules:
  0.0 129.5 jit_solution(6808596065469281502)
XLA Ops:
  0.6 0.0 copy-start.13
  2.0 0.0 copy-start.14
  2.0 0.0 copy-done.13
  2.0 0.7 copy-done.14
  2.6 0.0 copy-start.3
  2.6 0.9 copy-done.3
  3.6 0.0 copy-start.4
  3.6 0.9 copy-done.4
  4.5 0.0 copy-start.5
  4.5 0.9 copy-done.5
  5.4 0.0 copy-start.6
  5.4 0.9 copy-done.6
  6.3 0.0 copy-start.7
  6.3 0.9 copy-done.7
  7.3 0.0 copy-start.8
  7.3 0.9 copy-done.8
  8.2 0.0 copy-start.9
  8.2 0.9 copy-done.9
  9.1 0.0 copy-start.10
  9.1 0.8 copy-done.10
  9.9 0.0 copy-start.11
  9.9 0.8 copy-done.11
  10.7 0.0 copy-start.12
  10.7 0.8 copy-done.12
  11.5 0.0 copy-start.15
  11.5 1.0 copy-done.15
  12.6 82.3 %joint_backward.1 = (bf16[8,3072]{1,0:T(8,128)(2,1)S(1)}, bf16[2,32,3072]{2,1,0:T(8,128)(2,1)S(1)}, bf16[3,256,384]{2,1,0:T(8,128)(2,1)S(1)}) custom-call(s32[1]{0:T(128)S(6)} %copy.22.off_ref, s32[1]{0:T(128)S(6)} %copy.21.cnt_ref, bf16[8,3072]{1,0:T(8,128)(2,1)S(1)} %copy-done.10, bf16[8,3072]{1,0:T(8,128)(2,1)S(1)} %copy-done.11, ...), custom_call_target="tpu_custom_call" | custom-call | flops 2500000000 | bytes 4000000 | tf_op jit(solution)/shard_map/joint_backward/pallas_call | solution.py:604
  94.9 0.0 copy-start
  94.9 0.8 copy-done
  95.7 0.0 copy-start.1
  95.7 0.8 copy-done.1
  96.5 0.0 copy-start.2
  96.5 0.6 copy-done.2
  97.1 32.4 %deliver.1 = (bf16[8,3072]{1,0:T(8,128)(2,1)}, bf16[32,3072]{1,0:T(8,128)(2,1)}, bf16[32,3072]{1,0:T(8,128)(2,1)}, bf16[256,384]{1,0:T(8,128)(2,1)}, bf16[256,384]{1,0:T(8,128)(2,1)}, /*index=5*/bf16[256,384]{1,0:T(8,128)(2,1)}) custom-call(bf16[8,3072]{1,0:T(8,128)(2,1)} %copy-done.2, bf16[2,32,3072]{2,1,0:T(8,128)(2,1)} %copy-done.1, ...), custom_call_target="tpu_custom_call" | custom-call | tf_op jit(solution)/shard_map/deliver/pallas_call | solution.py:675
Async XLA Ops:
  0.6 1.3 %copy-start.13 = (f32[256,3]{0,1:T(4,128)S(1)}, f32[256,3]{0,1:T(4,128)}, u32[]{:S(2)}) copy-start(f32[256,3]{0,1:T(4,128)} %param.26) | copy-start | bytes 9220
  2.0 0.7 copy-start.14
  2.6 0.9 copy-start.3
  3.6 0.9 copy-start.4
  4.5 0.9 copy-start.5
  5.4 0.9 copy-start.6
  6.3 0.9 copy-start.7
  7.3 0.9 copy-start.8
  8.2 0.9 copy-start.9
  9.1 0.8 copy-start.10
  9.9 0.8 copy-start.11
  10.7 0.8 copy-start.12
  11.5 1.0 copy-start.15
  94.9 0.8 copy-start
  95.7 0.8 copy-start.1
  96.5 0.6 copy-start.2

commit v3 on v2

v3 whole, which is shorter than its diff:
```python
import jax
import jax.numpy as jnp
import numpy as np
from jax import lax
from jax.experimental import pallas as pl
from jax.experimental.pallas import tpu as pltpu
from jax.sharding import PartitionSpec as P

HEAD_DIM = 128
FACTOR = HEAD_DIM ** (-0.5)
NZ = 8
NX = 4
NB = NX * NX
HD = 3
W = HD * HEAD_DIM
ALL = NZ * W
TXT = 256
HALF = TXT // 2
ROWS = 64
KEYS = 256
SLAB_Q = NB * ROWS
STEP = 256
SILENT = 1e30
BF = jnp.bfloat16
F32 = jnp.float32
MESH = pl.DeviceIdType.MESH

TREE = (
    ((1, 0), (0, 0), (1, 0)),
    ((-1, 0), (0, 0), (-1, 0)),
    ((0, 1), (0, 0), (0, 1)),
    ((0, -1), (0, 0), (0, -1)),
    ((1, 1), (0, 0), (1, 1)),
    ((1, -1), (0, 0), (1, -1)),
    ((-1, 1), (0, 0), (-1, 1)),
    ((-1, -1), (0, 0), (-1, -1)),
    ((2, 0), (-1, 0), (-1, 0)),
    ((0, 2), (0, -1), (0, -1)),
    ((2, 1), (1, 1), (1, 0)),
    ((2, -1), (-1, -1), (-1, 0)),
    ((1, 2), (1, 1), (0, 1)),
    ((-1, 2), (-1, 1), (0, 1)),
    ((2, 2), (1, -1), (1, -1)),
)
EDGES = len(TREE)
BELOW = {child: [k for k, e in enumerate(TREE) if e[1] == child] for child, _, _ in TREE}
RELAYS = (1, 3, 4, 7, 6, 5)
LEAVES = (14, 8, 9, 10, 11, 12, 13, 0, 2)
AROUND = [e[2] for e in TREE[:8]]


def tables():
    place = np.arange(512, dtype=np.float64)[:, None]
    frequency = 10000.0 ** (-np.arange(32, dtype=np.float64) / 32)
    angles = np.tile(place * frequency[None, :], (1, 4))
    sign = np.where(np.arange(128) < 64, -1.0, 1.0)
    return np.stack([np.cos(angles), np.sin(angles) * sign]).astype(np.float32)


def nt(a, b):
    return lax.dot_general(a, b, (((1,), (1,)), ((), ())), preferred_element_type=F32)


def nn(a, b):
    return lax.dot_general(a, b, (((1,), (0,)), ((), ())), preferred_element_type=F32)


def turn(x, cosine, sine):
    return x * cosine + pltpu.roll(x, 64, 1) * sine


def turn_back(x, cosine, sine):
    return x * cosine - pltpu.roll(x, 64, 1) * sine


def cols(n):
    return slice(n * HEAD_DIM, (n + 1) * HEAD_DIM)


def attend(keys, keys_t, values, queries, cotan, logsum, delta, mask=None):
    p = jnp.exp(nt(keys, queries) * FACTOR - logsum)
    if mask is not None:
        p = p * mask
    dv = nn(p.astype(BF), cotan)
    dp = nt(values, cotan)
    ds = (p * (dp - delta) * FACTOR).astype(BF)
    return nn(keys_t, ds).T, nn(ds, queries), dv


def kernel(
    off_ref, cnt_ref, sq_h, so_h, sg_h, sl_h, ik_h, iv_h, tq_h, tk_h, tv_h, to_h, tg_h, tl_h, tab_h,
    sqo, okv, txo,
    sq, so, sg, sl, ik, iv, tq, tk, tv, to, tg, tl, tab,
    qgs, dls, qgr, dlr, kvs, kv, qg, st, stp, tkr, tst, qtk, dqt, dkvt, xt,
    dq, dkv, xk, dkvs, rs_s, rs_r, sqs, sqr, tx,
    s_in, s_z, r_zqg, r_zd, s_kv, r_kv, s_xy, r_xy, s_st, r_st, s_sib, r_sib, s_skv, r_skv, s_sd, r_sd,
    s_o, r_o, s_oq, r_oq, s_rs, r_rs, s_tx, r_tx,
):
    blk = lax.axis_index("blk")
    h = lax.axis_index("head")
    c = lax.rem(blk, 2)
    b = blk // 2
    bx = b // NX
    by = lax.rem(b, NX)
    lane = lax.broadcasted_iota(jnp.int32, (1, HEAD_DIM), 1)
    first = lax.rem(lane, 64) < 32
    sib = {"blk": 2 * b + 1 - c}

    def zdev(t):
        return lax.rem(h + t, NZ)

    def chip(dx, dy):
        return lax.rem(bx + dx + NX, NX) * NX + lax.rem(by + dy + NX, NX)

    def on_chip(e):
        return {"blk": 2 * e + c}

    def remote(src, dst, ss, rs, dev):
        return pltpu.make_async_remote_copy(
            src_ref=src, dst_ref=dst, send_sem=ss, recv_sem=rs, device_id=dev, device_id_type=MESH
        )

    def rows_of(e, count):
        return pl.ds(pl.multiple_of(e * count, count), count)

    def wide(d):
        return rows_of(d, W)

    def fetch(i, src, dst):
        copy = pltpu.make_async_copy(src, dst, s_in.at[i])
        copy.start()
        return copy

    f_slab = [fetch(1, sq_h, sq), fetch(2, sg_h, sg), fetch(3, so_h, so)]
    f_tab = fetch(0, tab_h, tab)
    f_k = fetch(4, ik_h, ik)
    f_v = fetch(5, iv_h, iv)
    f_text = [
        fetch(6, tq_h, tq), fetch(7, tg_h, tg), fetch(8, to_h, to), fetch(9, tk_h, tk),
        fetch(10, tv_h, tv), fetch(11, tl_h, tl), fetch(12, sl_h, sl),
    ]

    bar = pltpu.get_barrier_semaphore()

    def greet_z(t, carry):
        pl.semaphore_signal(bar, inc=1, device_id={"head": zdev(t)}, device_id_type=MESH)
        return carry

    lax.fori_loop(1, NZ, greet_z, 0)
    for dx, dy in AROUND:
        pl.semaphore_signal(bar, inc=1, device_id=on_chip(chip(dx, dy)), device_id_type=MESH)
    pl.semaphore_signal(bar, inc=1, device_id=sib, device_id_type=MESH)

    cos_t, sin_t = tab.at[0], tab.at[1]

    def angles(row, start, count):
        ct = cos_t[pl.ds(start, count), :]
        sn = sin_t[pl.ds(start, count), :]
        cr = cos_t[pl.ds(row, 1), :]
        sr = sin_t[pl.ds(row, 1), :]
        return jnp.where(first, cr, ct), jnp.where(first, sr, sn)

    place = off_ref[0] + blk
    row_at = lax.broadcasted_iota(jnp.int32, (32, 1), 0) == place // 4
    col_at = lax.rem(place, 4)

    def slab_angles(start, count):
        result = []
        for table in (cos_t, sin_t):
            row = jnp.sum(jnp.where(row_at, table[:32, :], 0.0), axis=0, keepdims=True)
            col = table[pl.ds(start, count), :]
            for i in range(1, 4):
                col = jnp.where(col_at == i, table[pl.ds(64 * i + start, count), :], col)
            result.append(jnp.where(first, row, col))
        return result

    f_tab.wait()
    for copy in f_slab:
        copy.wait()
    cq, sn_q = slab_angles(pl.multiple_of(8 * h, 8), 8)
    for d in range(NZ):
        acc = jnp.zeros((8, HEAD_DIM), F32)
        for j in range(HD):
            n = d * HD + j
            g = sg[:, cols(n)].astype(F32)
            q = turn(sq[:, cols(n)].astype(F32), cq, sn_q)
            qgs[d, :, cols(j)] = jnp.concatenate([q, g], axis=0).astype(BF)
            own = jnp.sum(g * so[:, cols(n)].astype(F32), axis=1, keepdims=True)
            acc = jnp.where(lane == j, own, acc)
        dls[d] = acc
    pl.semaphore_wait(bar, NZ + len(AROUND))

    def z_qg(t, d):
        return remote(qgs.at[d], qgr.at[h], s_z.at[0, t], r_zqg.at[h], {"head": d})

    def z_dl(t, d):
        return remote(dls.at[d], dlr.at[h], s_z.at[1, t], r_zd.at[h], {"head": d})

    def key_rows(s):
        return pl.ds(pl.multiple_of(c * KEYS + s * 32, 32), 32)

    def z_kv(j, t, d):
        return remote(
            kvs.at[d * HD + j], kv.at[j, :, key_rows(h), :], s_kv.at[j, t], r_kv.at[j, h], {"head": d}
        )

    def go_qg(t, carry):
        z_qg(t, zdev(t)).start()
        z_dl(t, zdev(t)).start()
        return carry

    lax.fori_loop(1, NZ, go_qg, 0)
    f_k.wait()
    f_v.wait()
    ck, sn_k = angles(blk, pl.multiple_of(32 * h, 32), 32)
    for j in range(HD):
        for d in range(NZ):
            n = d * HD + j
            kvs[n, 0] = turn(ik[:, cols(n)].astype(F32), ck, sn_k).astype(BF)
            kvs[n, 1] = iv[:, cols(n)]

        def go_kv(t, carry, j=j):
            z_kv(j, t, zdev(t)).start()
            return carry

        lax.fori_loop(1, NZ, go_kv, 0)
        kv[j, :, key_rows(h), :] = kvs[h * HD + j]
    qgr[h] = qgs[h]
    dlr[h] = dls[h]

    for copy in f_text:
        copy.wait()
    half = rows_of(c, HALF)
    text_at = pl.ds(pl.multiple_of(TXT + HALF * c, HALF), HALF)
    ct = cos_t[text_at, :]
    sn = sin_t[text_at, :]
    acc = jnp.zeros((HALF, HEAD_DIM), F32)
    for j in range(HD):
        g = tg[half, cols(j)]
        qg[j, 0, SLAB_Q:, :] = turn(tq[half, cols(j)].astype(F32), ct, sn).astype(BF)
        qg[j, 1, SLAB_Q:, :] = g
        own = jnp.sum(g.astype(F32) * to[half, cols(j)].astype(F32), axis=1, keepdims=True)
        acc = jnp.where(lane == j, own, acc)
        tkr[j] = turn(tk[:, cols(j)].astype(F32), cos_t[TXT:, :], sin_t[TXT:, :]).astype(BF)
    stp[:, SLAB_Q:] = acc.T[:8, :]
    stp[HD : 2 * HD, SLAB_Q:] = tl[:, half]

    def wait_qg(t, carry):
        s = zdev(t)
        remote(qgs.at[s], qgr.at[s], s_z.at[0, t], r_zqg.at[s], {"head": s}).wait_recv()
        remote(dls.at[s], dlr.at[s], s_z.at[1, t], r_zd.at[s], {"head": s}).wait_recv()
        return carry

    lax.fori_loop(1, NZ, wait_qg, 0)
    my_rows = rows_of(b, ROWS)
    odd = lax.rem(b, 2) == 1
    delta = dlr[...].reshape(ROWS, HEAD_DIM)
    blank = jnp.zeros_like(delta)
    spread = jnp.concatenate([jnp.where(odd, blank, delta), jnp.where(odd, delta, blank)], axis=0)
    here = (lane // 64) == lax.rem(b, 2)
    logs = jnp.concatenate([sl[...], sl[...]], axis=1)
    st[b] = spread.T[:8, :]
    st[b, HD : 2 * HD, :] = jnp.where(here, logs, 0.0)

    def ag(j, k, s, e):
        block = qg.at[j, :, rows_of(s, ROWS), :]
        return remote(block, block, s_xy.at[j, k], r_xy.at[j, k], on_chip(e))

    def ag_st(k, s, e):
        return remote(st.at[s], st.at[s], s_st.at[k], r_st.at[k], on_chip(e))

    def source(k):
        return chip(-TREE[k][0][0], -TREE[k][0][1])

    def from_parent(k, copy):
        _, (px, py), (dx, dy) = TREE[k]
        return copy(k, chip(-px, -py), chip(dx, dy))

    def ag_of(j):
        return lambda k, s, e: ag(j, k, s, e)

    for j in range(HD):
        both = qgr[:, :, cols(j)].astype(F32)
        qg[j, 0, my_rows, :] = both[:, :8, :].reshape(ROWS, HEAD_DIM).astype(BF)
        qg[j, 1, my_rows, :] = both[:, 8:, :].reshape(ROWS, HEAD_DIM).astype(BF)
        for k in range(8):
            if j == 0:
                from_parent(k, ag_st).start()
            from_parent(k, ag_of(j)).start()

    def ag_relay(j):
        for k in RELAYS:
            if j == 0:
                ag_st(k, source(k), b).wait_recv()
            ag(j, k, source(k), b).wait_recv()
            for child in BELOW[TREE[k][0]]:
                if j == 0:
                    from_parent(child, ag_st).start()
                from_parent(child, ag_of(j)).start()

    def ag_rest(j):
        for k in range(EDGES):
            if k not in RELAYS:
                if j == 0:
                    ag_st(k, source(k), b).wait_recv()
                ag(j, k, source(k), b).wait_recv()

    pair = pl.multiple_of(16 * (b // 2), 16)
    own_st = st[b]
    own_st = jnp.where(odd, pltpu.roll(own_st, 64, 1), own_st)
    text_st = pltpu.roll(stp[:, SLAB_Q:], lax.rem(ROWS - pair + HEAD_DIM, HEAD_DIM), 1)
    mine_at = lane // 8 == ROWS // 8 + lax.rem(b, 2)
    stat_row = lax.broadcasted_iota(jnp.int32, (8, 1), 0)
    silent = jnp.where(jnp.logical_and(stat_row >= HD, stat_row < 2 * HD), SILENT, 0.0)
    tst[...] = jnp.where(lane < ROWS, own_st, jnp.where(mine_at, text_st, silent))
    key_index = lax.broadcasted_iota(jnp.int32, (TXT, 1), 0)
    mask = (key_index < cnt_ref[0]).astype(F32)

    def text_keys(j):
        for i in range(2):
            qtk[i, :ROWS, :] = qg[j, i, my_rows, :]
            qtk[i, ROWS : ROWS + 16, :] = qg[j, i, pl.ds(SLAB_Q + pair, 16), :]
            qtk[i, ROWS + 16 :, :] = jnp.zeros((HEAD_DIM - ROWS - 16, HEAD_DIM), BF)
        keys = tkr[j]
        one_q, one_k, one_v = attend(
            keys, keys.T, tv[:, cols(j)], qtk[0], qtk[1],
            tst[HD + j : HD + j + 1, :], tst[j : j + 1, :], mask,
        )
        dqt[j] = one_q
        dkvt[j, 0] = one_k
        dkvt[j, 1] = one_v

    mine = rows_of(c, KEYS)
    theirs = rows_of(1 - c, KEYS)

    def sib_kv(j, rows):
        part = kv.at[j, :, rows, :]
        return remote(part, part, s_skv.at[j], r_skv.at[j], sib)

    def share_kv(j):
        def wait_kv(t, carry):
            s = zdev(t)
            remote(
                kvs.at[s * HD + j], kv.at[j, :, key_rows(s), :], s_kv.at[j, t], r_kv.at[j, s], {"head": s}
            ).wait_recv()
            return carry

        lax.fori_loop(1, NZ, wait_kv, 0)
        sib_kv(j, mine).start()

    text_keys(0)
    ag_relay(0)
    text_keys(1)
    share_kv(0)
    ag_relay(1)
    text_keys(2)
    other = rows_of(1 - c, HALF)
    sib_t = remote(dkvt.at[:, :, other, :], xt, s_sib.at[0], r_sib.at[0], sib)
    sib_t.start()
    ag_rest(0)
    for i in range(NB // 2):
        stp[:, cols(i)] = st[2 * i] + st[2 * i + 1]

    def image_keys(j, keys_t, rows, start):
        one_q, one_k, one_v = attend(
            kv[j, 0], keys_t, kv[j, 1], qg[j, 0, rows, :], qg[j, 1, rows, :],
            stp[HD + j : HD + j + 1, rows], stp[j : j + 1, rows],
        )
        dq[j, rows, :] = one_q
        if start:
            dkv[j, 0] = one_k
            dkv[j, 1] = one_v
        else:
            dkv[j, 0] += one_k
            dkv[j, 1] += one_v

    def sib_d(j):
        return remote(dkv.at[j, :, theirs, :], xk.at[j], s_sd.at[j], r_sd.at[j], sib)

    ck, sn_k = angles(blk, 0, KEYS)

    def token_rows(s):
        return rows_of(s, 32)

    def z_out(j, t, d):
        return remote(
            dkvs.at[j, :, token_rows(d), :], okv.at[h * HD + j], s_o.at[j, t], r_o.at[j, h], {"head": d}
        )

    def finish_kv(j):
        sib_d(j).wait()
        dkvs[j, 0] = turn_back(dkv[j, 0, mine, :] + xk[j, 0], ck, sn_k).astype(BF)
        dkvs[j, 1] = (dkv[j, 1, mine, :] + xk[j, 1]).astype(BF)

        def go_out(t, carry):
            z_out(j, t, zdev(t)).start()
            return carry

        lax.fori_loop(1, NZ, go_out, 0)
        okv[h * HD + j] = dkvs[j, :, token_rows(h), :]

    def own_rows(j, e):
        at = rows_of(e, 8)
        at_half = pl.ds(pl.multiple_of(HALF * c + e * 8, 8), 8)
        return jnp.concatenate(
            [
                dq[j, rows_of(e, ROWS), :],
                dq[j, pl.ds(pl.multiple_of(SLAB_Q + e * 8, 8), 8), :],
                dkvt[j, 0, at_half, :] + xt[j, 0, at, :],
                dkvt[j, 1, at_half, :] + xt[j, 1, at, :],
                jnp.zeros((8, HEAD_DIM), F32),
            ],
            axis=0,
        )

    def rs_copy(j, k):
        dx, dy = TREE[k][2]
        return remote(rs_s.at[j, k], rs_r.at[j, k], s_rs.at[j, k], r_rs.at[j, k], on_chip(chip(-dx, -dy)))

    def rs_gather(j, e, below):
        value = own_rows(j, e)
        for k in below:
            rs_copy(j, k).wait_recv()
            value = value + rs_r[j, k].astype(F32)
        return value

    def rs_pass(j, some):
        for k in some:
            rs_s[j, k] = rs_gather(j, source(k), BELOW[TREE[k][0]]).astype(BF)
            rs_copy(j, k).start()

    for j in range(HD):
        if j > 0:
            ag_rest(j)
        sib_kv(j, theirs).wait_recv()
        if j == 0:
            ag_relay(2)
        keys_t = kv[j, 0].T
        image_keys(j, keys_t, slice(SLAB_Q, SLAB_Q + HALF), True)
        for i in range(SLAB_Q // STEP):
            image_keys(j, keys_t, slice(i * STEP, (i + 1) * STEP), False)
        sib_d(j).start()
        if j == 0:
            sib_t.wait()
        if j < HD - 1:
            share_kv(j + 1)
        if j > 0:
            finish_kv(j - 1)
        rs_pass(j, LEAVES)
        if j > 0:
            rs_pass(j - 1, RELAYS)
    finish_kv(HD - 1)
    rs_pass(HD - 1, RELAYS)

    cq, sn_q = slab_angles(0, ROWS)
    own_at = pl.ds(pl.multiple_of(TXT + HALF * c + 8 * b, 8), 8)
    ct = cos_t[own_at, :]
    sn = sin_t[own_at, :]
    parts = []
    for j in range(HD):
        total = rs_gather(j, b, range(8))
        extra = jnp.where(odd, dqt[j, ROWS + 8 : ROWS + 16, :], dqt[j, ROWS : ROWS + 8, :])
        tx[c, b, :, cols(j)] = jnp.concatenate(
            [
                turn_back(total[ROWS : ROWS + 8, :] + extra, ct, sn),
                turn_back(total[ROWS + 8 : ROWS + 16, :], ct, sn),
                total[ROWS + 16 :, :],
            ],
            axis=0,
        ).astype(BF)
        parts.append(turn_back(total[:ROWS, :] + dqt[j, :ROWS, :], cq, sn_q).reshape(NZ, 8, HEAD_DIM))

    def tx_copy(k, s, e):
        return remote(tx.at[c, s], tx.at[c, s], s_tx.at[k], r_tx.at[k], on_chip(e))

    for k in range(8):
        from_parent(k, tx_copy).start()
    sqs[:, :, :HEAD_DIM] = jnp.concatenate([parts[0], parts[2]], axis=1).astype(BF)
    sqs[:, :, HEAD_DIM:] = jnp.concatenate([parts[1], jnp.zeros_like(parts[1])], axis=1).astype(BF)

    def out_q(t, d):
        return remote(sqs.at[d], sqr.at[h], s_oq.at[t], r_oq.at[h], {"head": d})

    def go_oq(t, carry):
        out_q(t, zdev(t)).start()
        return carry

    lax.fori_loop(1, NZ, go_oq, 0)
    sqr[h] = sqs[h]
    for k in RELAYS:
        tx_copy(k, source(k), b).wait_recv()
        for child in BELOW[TREE[k][0]]:
            from_parent(child, tx_copy).start()
    for k in range(EDGES):
        if k not in RELAYS:
            tx_copy(k, source(k), b).wait_recv()
    sib_tx = remote(tx.at[c], tx.at[c], s_sib.at[1], r_sib.at[1], sib)
    sib_tx.start()

    def wait_oq(t, carry):
        s = zdev(t)
        remote(sqs.at[s], sqr.at[s], s_oq.at[t], r_oq.at[s], {"head": s}).wait_recv()
        return carry

    lax.fori_loop(1, NZ, wait_oq, 0)
    for s in range(NZ):
        piece = sqr[s].astype(F32)
        sqo[:, s * W : s * W + 128] = piece[:8, :128].astype(BF)
        sqo[:, s * W + 128 : s * W + 256] = piece[:8, 128:].astype(BF)
        sqo[:, s * W + 256 : s * W + 384] = piece[8:, :128].astype(BF)
    remote(tx.at[1 - c], tx.at[1 - c], s_sib.at[1], r_sib.at[1], sib).wait_recv()
    for core in range(2):
        block = tx[core].astype(F32)
        rows = slice(core * HALF, (core + 1) * HALF)
        for i in range(3):
            txo[i, rows, :] = block[:, 8 * i : 8 * i + 8, :].reshape(HALF, W).astype(BF)
    for j in range(HD):

        def wait_out(t, carry, j=j):
            s = zdev(t)
            remote(
                dkvs.at[j, :, token_rows(s), :], okv.at[s * HD + j], s_o.at[j, t], r_o.at[j, s], {"head": s}
            ).wait_recv()
            return carry

        lax.fori_loop(1, NZ, wait_out, 0)

    def drain_z(t, carry):
        d = zdev(t)
        z_qg(t, d).wait_send()
        z_dl(t, d).wait_send()
        out_q(t, d).wait_send()
        for j in range(HD):
            z_kv(j, t, d).wait_send()
            z_out(j, t, d).wait_send()
        return carry

    lax.fori_loop(1, NZ, drain_z, 0)
    for k in range(EDGES):
        from_parent(k, ag_st).wait_send()
        from_parent(k, tx_copy).wait_send()
        for j in range(HD):
            from_parent(k, ag_of(j)).wait_send()
            rs_copy(j, k).wait_send()
    for j in range(HD):
        sib_kv(j, mine).wait_send()
    sib_tx.wait_send()


def deliver(sqo, okv, txo, sqg, ikg, ivg, tqg, tkg, tvg):
    sqg[...] = sqo[...]
    for n in range(NZ * HD):
        ikg[:, cols(n)] = okv[n, 0]
        ivg[:, cols(n)] = okv[n, 1]
    tqg[...] = txo[0]
    tkg[...] = txo[1]
    tvg[...] = txo[2]


def on_device(
    slab_query, slab_output, slab_cotangent, slab_logsum, image_keys, image_values,
    text_query, text_keys, text_values, text_output, text_cotangent, text_logsum,
    text_count, slab_offsets,
):
    vmem = pl.BlockSpec(memory_space=pltpu.VMEM)
    smem = pl.BlockSpec(memory_space=pltpu.SMEM)
    hbm = pl.BlockSpec(memory_space=pltpu.HBM)
    dma = pltpu.SemaphoreType.DMA
    slab = pltpu.VMEM((8, ALL), BF)
    text = pltpu.VMEM((TXT, W), BF)
    sqo, okv, txo = pl.pallas_call(
        kernel,
        out_shape=[
            jax.ShapeDtypeStruct((8, ALL), BF),
            jax.ShapeDtypeStruct((NZ * HD, 2, 32, HEAD_DIM), BF),
            jax.ShapeDtypeStruct((3, TXT, W), BF),
        ],
        in_specs=[smem, smem] + [hbm] * 13,
        out_specs=[vmem] * 3,
        scratch_shapes=[
            slab, slab, slab,
            pltpu.VMEM((HD, ROWS), F32),
            pltpu.VMEM((32, ALL), BF),
            pltpu.VMEM((32, ALL), BF),
            text, text, text, text, text,
            pltpu.VMEM((HD, TXT), F32),
            pltpu.VMEM((2, 512, HEAD_DIM), F32),
            pltpu.VMEM((NZ, 16, W), BF),
            pltpu.VMEM((NZ, 8, HEAD_DIM), F32),
            pltpu.VMEM((NZ, 16, W), BF),
            pltpu.VMEM((NZ, 8, HEAD_DIM), F32),
            pltpu.VMEM((NZ * HD, 2, 32, HEAD_DIM), BF),
            pltpu.VMEM((HD, 2, 2 * KEYS, HEAD_DIM), BF),
            pltpu.VMEM((HD, 2, SLAB_Q + HALF, HEAD_DIM), BF),
            pltpu.VMEM((NB, 8, HEAD_DIM), F32),
            pltpu.VMEM((8, SLAB_Q + HALF), F32),
            pltpu.VMEM((HD, TXT, HEAD_DIM), BF),
            pltpu.VMEM((8, HEAD_DIM), F32),
            pltpu.VMEM((2, HEAD_DIM, HEAD_DIM), BF),
            pltpu.VMEM((HD, HEAD_DIM, HEAD_DIM), F32),
            pltpu.VMEM((HD, 2, TXT, HEAD_DIM), F32),
            pltpu.VMEM((HD, 2, HALF, HEAD_DIM), F32),
            pltpu.VMEM((HD, SLAB_Q + HALF, HEAD_DIM), F32),
            pltpu.VMEM((HD, 2, 2 * KEYS, HEAD_DIM), F32),
            pltpu.VMEM((HD, 2, KEYS, HEAD_DIM), F32),
            pltpu.VMEM((HD, 2, KEYS, HEAD_DIM), BF),
            pltpu.VMEM((HD, EDGES, 96, HEAD_DIM), BF),
            pltpu.VMEM((HD, EDGES, 96, HEAD_DIM), BF),
            pltpu.VMEM((NZ, 16, 256), BF),
            pltpu.VMEM((NZ, 16, 256), BF),
            pltpu.VMEM((2, NB, 32, W), BF),
            dma((13,)),
            dma((2, NZ)), dma((NZ,)), dma((NZ,)),
            dma((HD, NZ)), dma((HD, NZ)),
            dma((HD, EDGES)), dma((HD, EDGES)),
            dma((EDGES,)), dma((EDGES,)),
            dma((2,)), dma((2,)),
            dma((HD,)), dma((HD,)), dma((HD,)), dma((HD,)),
            dma((HD, NZ)), dma((HD, NZ)),
            dma((NZ,)), dma((NZ,)),
            dma((HD, EDGES)), dma((HD, EDGES)),
            dma((EDGES,)), dma((EDGES,)),
        ],
        compiler_params=pltpu.CompilerParams(
            collective_id=0, has_side_effects=True, vmem_limit_bytes=63 * 1024 * 1024
        ),
        cost_estimate=pl.CostEstimate(
            flops=2_500_000_000, bytes_accessed=4_000_000, transcendentals=2_000_000
        ),
        name="joint_backward",
    )(
        slab_offsets, text_count, slab_query, slab_output, slab_cotangent, slab_logsum.T,
        image_keys, image_values, text_query, text_keys, text_values, text_output,
        text_cotangent, text_logsum.T, tables(),
    )
    shapes = [
        jax.ShapeDtypeStruct(x.shape, BF)
        for x in (slab_query, image_keys, image_values, text_query, text_keys, text_values)
    ]
    return pl.pallas_call(
        deliver, out_shape=shapes, in_specs=[vmem] * 3, out_specs=[vmem] * 6, name="deliver"
    )(sqo, okv, txo)


def solution(mesh):
    tokens = P(("rep", "blk", "head"), None)
    text = P("rep", "head")
    in_specs = (
        tokens, tokens, tokens, P(("rep", "blk"), "head"), tokens, tokens,
        text, text, text, text, text, text, P("rep"), P("rep"),
    )
    out_specs = (tokens, tokens, tokens, text, text, text)
    return jax.shard_map(
        on_device, mesh=mesh, in_specs=in_specs, out_specs=out_specs, check_vma=False
    )
```

time: 130 us -> 74.8 us (0.58)
  the two profiles are of different devices: /device:TPU:131 before, /device:TPU:1 now
where the time goes in v3:
time: 74.8 us; the launch traced here: 74.7 us
  Pallas kernels  72.7 us (97%)
  between operations  1.94 us (3%)
    pallas_call x1, Pallas kernels, on_device(): pl.pallas_call(kernel, out_shape=[jax.ShapeDtypeStruct((8, ALL), BF), jax...  70.5 us
    pallas_call x1, Pallas kernels, on_device(): pl.pallas_call(deliver, out_shape=shapes, in_specs=[vmem] * 3, out_specs=...  2.2 us

profile of v3, /device:TPU:1, one launch (start us, length us, event | category | flops | bytes accessed | tf_op | source)
XLA Modules:
  0.0 74.7 jit_solution(7864705333585177459)
XLA Ops:
  1.9 70.5 %joint_backward.1 = (bf16[8,3072]{1,0:T(8,128)(2,1)}, bf16[24,2,32,128]{3,2,1,0:T(8,128)(2,1)}, bf16[3,256,384]{2,1,0:T(8,128)(2,1)}) custom-call(s32[1]{0:T(128)S(6)} %copy.22.off_ref, s32[1]{0:T(128)S(6)} %copy.21.cnt_ref, bf16[8,3072]{1,0:T(8,128)(2,1)} %sq_h.1, bf16[8,3072]{1,0:T(8,128)(2,1)} %so_h.1, bf16[8,3072]{1,0:T(8,128)(2,1)} %sg_h.1, ...), custom_call_target="tpu_custom_call" | custom-call | flops 2500000000 | bytes 4000000 | tf_op jit(solution)/shard_map/joint_backward/pallas_call | solution.py:571
  72.5 2.2 %deliver.1 = (bf16[8,3072]{1,0:T(8,128)(2,1)}, bf16[32,3072]{1,0:T(8,128)(2,1)}, bf16[32,3072]{1,0:T(8,128)(2,1)}, bf16[256,384]{1,0:T(8,128)(2,1)}, bf16[256,384]{1,0:T(8,128)(2,1)}, /*index=5*/bf16[256,384]{1,0:T(8,128)(2,1)}) custom-call(bf16[8,3072]{1,0:T(8,128)(2,1)} %get-tuple-element.9.sqo, bf16[24,2,32,128]{3,2,1,0:T(8,128)(2,1)} %get-tuple-element.10.okv, ...), custom_call_target="tpu_custom_call" | custom-call | tf_op jit(solution)/shard_map/deliver/pallas_call | solution.py:640

commit v4 on v3

--- a/solution.py
+++ b/solution.py
@@ -92,9 +92,9 @@
     sqo, okv, txo,
     sq, so, sg, sl, ik, iv, tq, tk, tv, to, tg, tl, tab,
     qgs, dls, qgr, dlr, kvs, kv, qg, st, stp, tkr, tst, qtk, dqt, dkvt, xt,
-    dq, dkv, xk, dkvs, rs_s, rs_r, sqs, sqr, tx,
+    dq, dkv, xs, xk, dkvs, rs_s, rs_r, tk_s, tk_r, sqs, sqr, tx, tkx,
     s_in, s_z, r_zqg, r_zd, s_kv, r_kv, s_xy, r_xy, s_st, r_st, s_sib, r_sib, s_skv, r_skv, s_sd, r_sd,
-    s_o, r_o, s_oq, r_oq, s_rs, r_rs, s_tx, r_tx,
+    s_o, r_o, s_oq, r_oq, s_rs, r_rs, s_tx, r_tx, s_tk, r_tk, s_tkx, r_tkx,
 ):
     blk = lax.axis_index("blk")
     h = lax.axis_index("head")
@@ -103,6 +103,7 @@
     bx = b // NX
     by = lax.rem(b, NX)
     lane = lax.broadcasted_iota(jnp.int32, (1, HEAD_DIM), 1)
+    sub = lax.broadcasted_iota(jnp.int32, (8, 1), 0)
     first = lax.rem(lane, 64) < 32
     sib = {"blk": 2 * b + 1 - c}
 
@@ -186,8 +187,8 @@
             q = turn(sq[:, cols(n)].astype(F32), cq, sn_q)
             qgs[d, :, cols(j)] = jnp.concatenate([q, g], axis=0).astype(BF)
             own = jnp.sum(g * so[:, cols(n)].astype(F32), axis=1, keepdims=True)
-            acc = jnp.where(lane == j, own, acc)
-        dls[d] = acc
+            acc = jnp.where(lane == 8 * j + sub, own, acc)
+        dls[d] = jnp.sum(acc, axis=0, keepdims=True)
     pl.semaphore_wait(bar, NZ + len(AROUND))
 
     def z_qg(t, d):
@@ -254,12 +255,17 @@
     lax.fori_loop(1, NZ, wait_qg, 0)
     my_rows = rows_of(b, ROWS)
     odd = lax.rem(b, 2) == 1
-    delta = dlr[...].reshape(ROWS, HEAD_DIM)
-    blank = jnp.zeros_like(delta)
-    spread = jnp.concatenate([jnp.where(odd, blank, delta), jnp.where(odd, delta, blank)], axis=0)
+    delta = dlr[...].reshape(NZ, HEAD_DIM)
+    shift = ROWS * lax.rem(b, 2)
     here = (lane // 64) == lax.rem(b, 2)
     logs = jnp.concatenate([sl[...], sl[...]], axis=1)
-    st[b] = spread.T[:8, :]
+    st[b] = jnp.zeros((8, HEAD_DIM), F32)
+    moved = [pltpu.roll(delta[i : i + 1, :], 8 * i, 1) if i else delta[:1, :] for i in range(NZ)]
+    for j in range(HD):
+        row = jnp.zeros((1, HEAD_DIM), F32)
+        for i in range(NZ):
+            row = jnp.where(lane // 8 == i + j, moved[i], row)
+        st[b, j : j + 1, :] = pltpu.roll(row, lax.rem(shift + HEAD_DIM - 8 * j, HEAD_DIM), 1)
     st[b, HD : 2 * HD, :] = jnp.where(here, logs, 0.0)
 
     def ag(j, k, s, e):
@@ -375,7 +381,7 @@
             dkv[j, 1] += one_v
 
     def sib_d(j):
-        return remote(dkv.at[j, :, theirs, :], xk.at[j], s_sd.at[j], r_sd.at[j], sib)
+        return remote(xs.at[j], xk.at[j], s_sd.at[j], r_sd.at[j], sib)
 
     ck, sn_k = angles(blk, 0, KEYS)
 
@@ -389,8 +395,8 @@
 
     def finish_kv(j):
         sib_d(j).wait()
-        dkvs[j, 0] = turn_back(dkv[j, 0, mine, :] + xk[j, 0], ck, sn_k).astype(BF)
-        dkvs[j, 1] = (dkv[j, 1, mine, :] + xk[j, 1]).astype(BF)
+        dkvs[j, 0] = turn_back(dkv[j, 0, mine, :] + xk[j, 0].astype(F32), ck, sn_k).astype(BF)
+        dkvs[j, 1] = (dkv[j, 1, mine, :] + xk[j, 1].astype(F32)).astype(BF)
 
         def go_out(t, carry):
             z_out(j, t, zdev(t)).start()
@@ -399,36 +405,90 @@
         lax.fori_loop(1, NZ, go_out, 0)
         okv[h * HD + j] = dkvs[j, :, token_rows(h), :]
 
-    def own_rows(j, e):
+    def make_sum(own, copy, sent, got):
+        def gather(e, below):
+            value = own(e)
+            for k in below:
+                copy(k).wait_recv()
+                value = value + got[k].astype(F32)
+            return value
+
+        def pass_on(some):
+            for k in some:
+                sent[k] = gather(source(k), BELOW[TREE[k][0]]).astype(BF)
+                copy(k).start()
+
+        return gather, pass_on
+
+    def towards_root(k, src, dst, ss, rs):
+        dx, dy = TREE[k][2]
+        return remote(src, dst, ss, rs, on_chip(chip(-dx, -dy)))
+
+    def rs_copy(j, k):
+        return towards_root(k, rs_s.at[j, k], rs_r.at[j, k], s_rs.at[j, k], r_rs.at[j, k])
+
+    def tk_copy(k):
+        return towards_root(k, tk_s.at[k], tk_r.at[k], s_tk.at[k], r_tk.at[k])
+
+    def own_rows(j):
+        def own(e):
+            text = dq[j, pl.ds(pl.multiple_of(SLAB_Q + e * 8, 8), 8), :]
+            return jnp.concatenate([dq[j, rows_of(e, ROWS), :], text, jnp.zeros_like(text)], axis=0)
+
+        return own
+
+    def own_text(e):
         at = rows_of(e, 8)
         at_half = pl.ds(pl.multiple_of(HALF * c + e * 8, 8), 8)
-        return jnp.concatenate(
-            [
-                dq[j, rows_of(e, ROWS), :],
-                dq[j, pl.ds(pl.multiple_of(SLAB_Q + e * 8, 8), 8), :],
-                dkvt[j, 0, at_half, :] + xt[j, 0, at, :],
-                dkvt[j, 1, at_half, :] + xt[j, 1, at, :],
-                jnp.zeros((8, HEAD_DIM), F32),
-            ],
-            axis=0,
-        )
-
-    def rs_copy(j, k):
-        dx, dy = TREE[k][2]
-        return remote(rs_s.at[j, k], rs_r.at[j, k], s_rs.at[j, k], r_rs.at[j, k], on_chip(chip(-dx, -dy)))
-
-    def rs_gather(j, e, below):
-        value = own_rows(j, e)
-        for k in below:
-            rs_copy(j, k).wait_recv()
-            value = value + rs_r[j, k].astype(F32)
-        return value
-
-    def rs_pass(j, some):
-        for k in some:
-            rs_s[j, k] = rs_gather(j, source(k), BELOW[TREE[k][0]]).astype(BF)
-            rs_copy(j, k).start()
-
+        heads = [
+            jnp.concatenate([dkvt[j, i, at_half, :] + xt[j, i, at, :] for i in range(2)], axis=0)
+            for j in range(HD)
+        ]
+        return jnp.concatenate(heads, axis=1)
+
+    rs_sums = [
+        make_sum(own_rows(j), lambda k, j=j: rs_copy(j, k), rs_s.at[j], rs_r.at[j]) for j in range(HD)
+    ]
+    tk_gather, tk_pass = make_sum(own_text, tk_copy, tk_s, tk_r)
+
+    def tx_copy(k, s, e):
+        return remote(tx.at[c, s], tx.at[c, s], s_tx.at[k], r_tx.at[k], on_chip(e))
+
+    def tkx_copy(k, s, e):
+        return remote(tkx.at[c, s], tkx.at[c, s], s_tkx.at[k], r_tkx.at[k], on_chip(e))
+
+    def spread_out(copy):
+        for k in range(8):
+            from_parent(k, copy).start()
+
+    def spread_on(copy):
+        for k in RELAYS:
+            copy(k, source(k), b).wait_recv()
+            for child in BELOW[TREE[k][0]]:
+                from_parent(child, copy).start()
+
+    def spread_end(copy):
+        for k in range(EDGES):
+            if k not in RELAYS:
+                copy(k, source(k), b).wait_recv()
+
+    own_at = pl.ds(pl.multiple_of(TXT + HALF * c + 8 * b, 8), 8)
+    ct = cos_t[own_at, :]
+    sn = sin_t[own_at, :]
+
+    def text_key_result():
+        total = tk_gather(b, range(8))
+        for j in range(HD):
+            tkx[c, b, :, cols(j)] = jnp.concatenate(
+                [turn_back(total[:8, cols(j)], ct, sn), total[8:, cols(j)]], axis=0
+            ).astype(BF)
+        spread_out(tkx_copy)
+
+    sib_tkx = remote(tkx.at[c], tkx.at[c], s_sib.at[2], r_sib.at[2], sib)
+    sib_tx = remote(tx.at[c], tx.at[c], s_sib.at[1], r_sib.at[1], sib)
+
+    sib_t.wait()
+    tk_pass(LEAVES)
     for j in range(HD):
         if j > 0:
             ag_rest(j)
@@ -439,42 +499,37 @@
         image_keys(j, keys_t, slice(SLAB_Q, SLAB_Q + HALF), True)
         for i in range(SLAB_Q // STEP):
             image_keys(j, keys_t, slice(i * STEP, (i + 1) * STEP), False)
+            if i == 1 and j > 0:
+                finish_kv(j - 1)
+        xs[j] = dkv[j, :, theirs, :].astype(BF)
         sib_d(j).start()
-        if j == 0:
-            sib_t.wait()
         if j < HD - 1:
             share_kv(j + 1)
-        if j > 0:
-            finish_kv(j - 1)
-        rs_pass(j, LEAVES)
-        if j > 0:
-            rs_pass(j - 1, RELAYS)
+        rs_sums[j][1](LEAVES)
+        if j == 0:
+            tk_pass(RELAYS)
+        else:
+            rs_sums[j - 1][1](RELAYS)
+        if j == 1:
+            text_key_result()
+        if j == 2:
+            spread_on(tkx_copy)
     finish_kv(HD - 1)
-    rs_pass(HD - 1, RELAYS)
+    rs_sums[HD - 1][1](RELAYS)
 
     cq, sn_q = slab_angles(0, ROWS)
-    own_at = pl.ds(pl.multiple_of(TXT + HALF * c + 8 * b, 8), 8)
-    ct = cos_t[own_at, :]
-    sn = sin_t[own_at, :]
     parts = []
+    text_parts = []
     for j in range(HD):
-        total = rs_gather(j, b, range(8))
+        total = rs_sums[j][0](b, range(8))
         extra = jnp.where(odd, dqt[j, ROWS + 8 : ROWS + 16, :], dqt[j, ROWS : ROWS + 8, :])
-        tx[c, b, :, cols(j)] = jnp.concatenate(
-            [
-                turn_back(total[ROWS : ROWS + 8, :] + extra, ct, sn),
-                turn_back(total[ROWS + 8 : ROWS + 16, :], ct, sn),
-                total[ROWS + 16 :, :],
-            ],
-            axis=0,
-        ).astype(BF)
+        text_parts.append(turn_back(total[ROWS : ROWS + 8, :] + extra, ct, sn))
         parts.append(turn_back(total[:ROWS, :] + dqt[j, :ROWS, :], cq, sn_q).reshape(NZ, 8, HEAD_DIM))
-
-    def tx_copy(k, s, e):
-        return remote(tx.at[c, s], tx.at[c, s], s_tx.at[k], r_tx.at[k], on_chip(e))
-
-    for k in range(8):
-        from_parent(k, tx_copy).start()
+    tx[c, b, :, :HEAD_DIM] = jnp.concatenate([text_parts[0], text_parts[2]], axis=0).astype(BF)
+    tx[c, b, :, HEAD_DIM:] = jnp.concatenate(
+        [text_parts[1], jnp.zeros_like(text_parts[1])], axis=0
+    ).astype(BF)
+    spread_out(tx_copy)
     sqs[:, :, :HEAD_DIM] = jnp.concatenate([parts[0], parts[2]], axis=1).astype(BF)
     sqs[:, :, HEAD_DIM:] = jnp.concatenate([parts[1], jnp.zeros_like(parts[1])], axis=1).astype(BF)
 
@@ -487,14 +542,10 @@
 
     lax.fori_loop(1, NZ, go_oq, 0)
     sqr[h] = sqs[h]
-    for k in RELAYS:
-        tx_copy(k, source(k), b).wait_recv()
-        for child in BELOW[TREE[k][0]]:
-            from_parent(child, tx_copy).start()
-    for k in range(EDGES):
-        if k not in RELAYS:
-            tx_copy(k, source(k), b).wait_recv()
-    sib_tx = remote(tx.at[c], tx.at[c], s_sib.at[1], r_sib.at[1], sib)
+    spread_end(tkx_copy)
+    sib_tkx.start()
+    spread_on(tx_copy)
+    spread_end(tx_copy)
     sib_tx.start()
 
     def wait_oq(t, carry):
@@ -508,12 +559,19 @@
         sqo[:, s * W : s * W + 128] = piece[:8, :128].astype(BF)
         sqo[:, s * W + 128 : s * W + 256] = piece[:8, 128:].astype(BF)
         sqo[:, s * W + 256 : s * W + 384] = piece[8:, :128].astype(BF)
+    remote(tkx.at[1 - c], tkx.at[1 - c], s_sib.at[2], r_sib.at[2], sib).wait_recv()
+    for core in range(2):
+        rows = slice(core * HALF, (core + 1) * HALF)
+        block = tkx[core].astype(F32)
+        txo[1, rows, :] = block[:, :8, :].reshape(HALF, W).astype(BF)
+        txo[2, rows, :] = block[:, 8:, :].reshape(HALF, W).astype(BF)
     remote(tx.at[1 - c], tx.at[1 - c], s_sib.at[1], r_sib.at[1], sib).wait_recv()
     for core in range(2):
+        rows = slice(core * HALF, (core + 1) * HALF)
         block = tx[core].astype(F32)
-        rows = slice(core * HALF, (core + 1) * HALF)
-        for i in range(3):
-            txo[i, rows, :] = block[:, 8 * i : 8 * i + 8, :].reshape(HALF, W).astype(BF)
+        txo[0, rows, :HEAD_DIM] = block[:, :8, :HEAD_DIM].reshape(HALF, HEAD_DIM).astype(BF)
+        txo[0, rows, HEAD_DIM : 2 * HEAD_DIM] = block[:, :8, HEAD_DIM:].reshape(HALF, HEAD_DIM).astype(BF)
+        txo[0, rows, 2 * HEAD_DIM :] = block[:, 8:, :HEAD_DIM].reshape(HALF, HEAD_DIM).astype(BF)
     for j in range(HD):
 
         def wait_out(t, carry, j=j):
@@ -539,12 +597,15 @@
     for k in range(EDGES):
         from_parent(k, ag_st).wait_send()
         from_parent(k, tx_copy).wait_send()
+        from_parent(k, tkx_copy).wait_send()
+        tk_copy(k).wait_send()
         for j in range(HD):
             from_parent(k, ag_of(j)).wait_send()
             rs_copy(j, k).wait_send()
     for j in range(HD):
         sib_kv(j, mine).wait_send()
     sib_tx.wait_send()
+    sib_tkx.wait_send()
 
 
 def deliver(sqo, okv, txo, sqg, ikg, ivg, tqg, tkg, tvg):
@@ -586,9 +647,9 @@
             pltpu.VMEM((HD, TXT), F32),
             pltpu.VMEM((2, 512, HEAD_DIM), F32),
             pltpu.VMEM((NZ, 16, W), BF),
-            pltpu.VMEM((NZ, 8, HEAD_DIM), F32),
+            pltpu.VMEM((NZ, 1, HEAD_DIM), F32),
             pltpu.VMEM((NZ, 16, W), BF),
-            pltpu.VMEM((NZ, 8, HEAD_DIM), F32),
+            pltpu.VMEM((NZ, 1, HEAD_DIM), F32),
             pltpu.VMEM((NZ * HD, 2, 32, HEAD_DIM), BF),
             pltpu.VMEM((HD, 2, 2 * KEYS, HEAD_DIM), BF),
             pltpu.VMEM((HD, 2, SLAB_Q + HALF, HEAD_DIM), BF),
@@ -602,23 +663,29 @@
             pltpu.VMEM((HD, 2, HALF, HEAD_DIM), F32),
             pltpu.VMEM((HD, SLAB_Q + HALF, HEAD_DIM), F32),
             pltpu.VMEM((HD, 2, 2 * KEYS, HEAD_DIM), F32),
-            pltpu.VMEM((HD, 2, KEYS, HEAD_DIM), F32),
             pltpu.VMEM((HD, 2, KEYS, HEAD_DIM), BF),
-            pltpu.VMEM((HD, EDGES, 96, HEAD_DIM), BF),
-            pltpu.VMEM((HD, EDGES, 96, HEAD_DIM), BF),
+            pltpu.VMEM((HD, 2, KEYS, HEAD_DIM), BF),
+            pltpu.VMEM((HD, 2, KEYS, HEAD_DIM), BF),
+            pltpu.VMEM((HD, EDGES, 80, HEAD_DIM), BF),
+            pltpu.VMEM((HD, EDGES, 80, HEAD_DIM), BF),
+            pltpu.VMEM((EDGES, 16, W), BF),
+            pltpu.VMEM((EDGES, 16, W), BF),
             pltpu.VMEM((NZ, 16, 256), BF),
             pltpu.VMEM((NZ, 16, 256), BF),
-            pltpu.VMEM((2, NB, 32, W), BF),
+            pltpu.VMEM((2, NB, 16, 256), BF),
+            pltpu.VMEM((2, NB, 16, W), BF),
             dma((13,)),
             dma((2, NZ)), dma((NZ,)), dma((NZ,)),
             dma((HD, NZ)), dma((HD, NZ)),
             dma((HD, EDGES)), dma((HD, EDGES)),
             dma((EDGES,)), dma((EDGES,)),
-            dma((2,)), dma((2,)),
+            dma((3,)), dma((3,)),
             dma((HD,)), dma((HD,)), dma((HD,)), dma((HD,)),
             dma((HD, NZ)), dma((HD, NZ)),
             dma((NZ,)), dma((NZ,)),
             dma((HD, EDGES)), dma((HD, EDGES)),
+            dma((EDGES,)), dma((EDGES,)),
+            dma((EDGES,)), dma((EDGES,)),
             dma((EDGES,)), dma((EDGES,)),
         ],
         compiler_params=pltpu.CompilerParams(

time: 74.8 us -> 73.6 us (0.984)
  Pallas kernels: 72.7 us -> 71.5 us
    pallas_call x1, Pallas kernels: 70.5 us -> 69.3 us  [on_device(): pl.pallas_call(kernel, out_shape=[jax.ShapeDtypeStruct((8, ALL), BF), jax...]
where the time goes in v4:
time: 73.6 us; the launch traced here: 73.4 us
  Pallas kernels  71.5 us (97%)
  between operations  1.94 us (3%)
    pallas_call x1, Pallas kernels, on_device(): pl.pallas_call(kernel, out_shape=[jax.ShapeDtypeStruct((8, ALL), BF), jax...  69.3 us
    pallas_call x1, Pallas kernels, on_device(): pl.pallas_call(deliver, out_shape=shapes, in_specs=[vmem] * 3, out_specs=...  2.2 us

profile of v4, /device:TPU:1, one launch (start us, length us, event | category | flops | bytes accessed | tf_op | source)
XLA Modules:
  0.0 73.4 jit_solution(8278654979366234979)
XLA Ops:
  1.9 69.3 %joint_backward.1 = (bf16[8,3072]{1,0:T(8,128)(2,1)}, bf16[24,2,32,128]{3,2,1,0:T(8,128)(2,1)}, bf16[3,256,384]{2,1,0:T(8,128)(2,1)}) custom-call(s32[1]{0:T(128)S(6)} %copy.22.off_ref, s32[1]{0:T(128)S(6)} %copy.21.cnt_ref, bf16[8,3072]{1,0:T(8,128)(2,1)} %sq_h.1, bf16[8,3072]{1,0:T(8,128)(2,1)} %so_h.1, bf16[8,3072]{1,0:T(8,128)(2,1)} %sg_h.1, ...), custom_call_target="tpu_custom_call" | custom-call | flops 2500000000 | bytes 4000000 | tf_op jit(solution)/shard_map/joint_backward/pallas_call | solution.py:632
  71.2 2.2 %deliver.1 = (bf16[8,3072]{1,0:T(8,128)(2,1)}, bf16[32,3072]{1,0:T(8,128)(2,1)}, bf16[32,3072]{1,0:T(8,128)(2,1)}, bf16[256,384]{1,0:T(8,128)(2,1)}, bf16[256,384]{1,0:T(8,128)(2,1)}, /*index=5*/bf16[256,384]{1,0:T(8,128)(2,1)}) custom-call(bf16[8,3072]{1,0:T(8,128)(2,1)} %get-tuple-element.9.sqo, bf16[24,2,32,128]{3,2,1,0:T(8,128)(2,1)} %get-tuple-element.10.okv, ...), custom_call_target="tpu_custom_call" | custom-call | tf_op jit(solution)/shard_map/deliver/pallas_call | solution.py:707

commit v5 on v4

--- a/solution.py
+++ b/solution.py
@@ -107,8 +107,12 @@
     first = lax.rem(lane, 64) < 32
     sib = {"blk": 2 * b + 1 - c}
 
+    side = h // (NZ // 2)
+
     def zdev(t):
-        return lax.rem(h + t, NZ)
+        over = (1 - side) * (NZ // 2) + lax.rem(h + t, NZ // 2)
+        near = side * (NZ // 2) + lax.rem(h + t, NZ // 2)
+        return jnp.where(t <= NZ // 2, over, near)
 
     def chip(dx, dy):
         return lax.rem(bx + dx + NX, NX) * NX + lax.rem(by + dy + NX, NX)
@@ -501,47 +505,54 @@
             image_keys(j, keys_t, slice(i * STEP, (i + 1) * STEP), False)
             if i == 1 and j > 0:
                 finish_kv(j - 1)
+        if j == HD - 1:
+            rs_sums[j][1](LEAVES)
         xs[j] = dkv[j, :, theirs, :].astype(BF)
         sib_d(j).start()
-        if j < HD - 1:
-            share_kv(j + 1)
-        rs_sums[j][1](LEAVES)
         if j == 0:
+            share_kv(1)
+            rs_sums[0][1](LEAVES)
             tk_pass(RELAYS)
+        elif j == 1:
+            rs_sums[1][1](LEAVES)
+            rs_sums[0][1](RELAYS)
+            share_kv(2)
+            text_key_result()
         else:
-            rs_sums[j - 1][1](RELAYS)
-        if j == 1:
-            text_key_result()
-        if j == 2:
-            spread_on(tkx_copy)
+            rs_sums[1][1](RELAYS)
+
+    cq, sn_q = slab_angles(0, ROWS)
+
+    def own_result(j):
+        total = rs_sums[j][0](b, range(8))
+        extra = jnp.where(odd, dqt[j, ROWS + 8 : ROWS + 16, :], dqt[j, ROWS : ROWS + 8, :])
+        text = turn_back(total[ROWS : ROWS + 8, :] + extra, ct, sn)
+        return turn_back(total[:ROWS, :] + dqt[j, :ROWS, :], cq, sn_q).reshape(NZ, 8, HEAD_DIM), text
+
+    def out_q(i, t, d):
+        return remote(sqs.at[d, i], sqr.at[h, i], s_oq.at[i, t], r_oq.at[i, h], {"head": d})
+
+    def send_q(i):
+        def go_oq(t, carry):
+            out_q(i, t, zdev(t)).start()
+            return carry
+
+        lax.fori_loop(1, NZ, go_oq, 0)
+        sqr[h, i] = sqs[h, i]
+
+    part_0, text_0 = own_result(0)
     finish_kv(HD - 1)
     rs_sums[HD - 1][1](RELAYS)
-
-    cq, sn_q = slab_angles(0, ROWS)
-    parts = []
-    text_parts = []
-    for j in range(HD):
-        total = rs_sums[j][0](b, range(8))
-        extra = jnp.where(odd, dqt[j, ROWS + 8 : ROWS + 16, :], dqt[j, ROWS : ROWS + 8, :])
-        text_parts.append(turn_back(total[ROWS : ROWS + 8, :] + extra, ct, sn))
-        parts.append(turn_back(total[:ROWS, :] + dqt[j, :ROWS, :], cq, sn_q).reshape(NZ, 8, HEAD_DIM))
-    tx[c, b, :, :HEAD_DIM] = jnp.concatenate([text_parts[0], text_parts[2]], axis=0).astype(BF)
-    tx[c, b, :, HEAD_DIM:] = jnp.concatenate(
-        [text_parts[1], jnp.zeros_like(text_parts[1])], axis=0
-    ).astype(BF)
+    part_1, text_1 = own_result(1)
+    sqs[:, 0] = jnp.concatenate([part_0, part_1], axis=1).astype(BF)
+    send_q(0)
+    spread_on(tkx_copy)
+    part_2, text_2 = own_result(2)
+    sqs[:, 1] = jnp.concatenate([part_2, jnp.zeros_like(part_2)], axis=1).astype(BF)
+    send_q(1)
+    tx[c, b, :, :HEAD_DIM] = jnp.concatenate([text_0, text_2], axis=0).astype(BF)
+    tx[c, b, :, HEAD_DIM:] = jnp.concatenate([text_1, jnp.zeros_like(text_1)], axis=0).astype(BF)
     spread_out(tx_copy)
-    sqs[:, :, :HEAD_DIM] = jnp.concatenate([parts[0], parts[2]], axis=1).astype(BF)
-    sqs[:, :, HEAD_DIM:] = jnp.concatenate([parts[1], jnp.zeros_like(parts[1])], axis=1).astype(BF)
-
-    def out_q(t, d):
-        return remote(sqs.at[d], sqr.at[h], s_oq.at[t], r_oq.at[h], {"head": d})
-
-    def go_oq(t, carry):
-        out_q(t, zdev(t)).start()
-        return carry
-
-    lax.fori_loop(1, NZ, go_oq, 0)
-    sqr[h] = sqs[h]
     spread_end(tkx_copy)
     sib_tkx.start()
     spread_on(tx_copy)
@@ -550,15 +561,15 @@
 
     def wait_oq(t, carry):
         s = zdev(t)
-        remote(sqs.at[s], sqr.at[s], s_oq.at[t], r_oq.at[s], {"head": s}).wait_recv()
+        for i in range(2):
+            remote(sqs.at[s, i], sqr.at[s, i], s_oq.at[i, t], r_oq.at[i, s], {"head": s}).wait_recv()
         return carry
 
     lax.fori_loop(1, NZ, wait_oq, 0)
     for s in range(NZ):
         piece = sqr[s].astype(F32)
-        sqo[:, s * W : s * W + 128] = piece[:8, :128].astype(BF)
-        sqo[:, s * W + 128 : s * W + 256] = piece[:8, 128:].astype(BF)
-        sqo[:, s * W + 256 : s * W + 384] = piece[8:, :128].astype(BF)
+        for j in range(HD):
+            sqo[:, cols(s * HD + j)] = piece[j // 2, 8 * (j % 2) : 8 * (j % 2) + 8, :].astype(BF)
     remote(tkx.at[1 - c], tkx.at[1 - c], s_sib.at[2], r_sib.at[2], sib).wait_recv()
     for core in range(2):
         rows = slice(core * HALF, (core + 1) * HALF)
@@ -587,7 +598,8 @@
         d = zdev(t)
         z_qg(t, d).wait_send()
         z_dl(t, d).wait_send()
-        out_q(t, d).wait_send()
+        out_q(0, t, d).wait_send()
+        out_q(1, t, d).wait_send()
         for j in range(HD):
             z_kv(j, t, d).wait_send()
             z_out(j, t, d).wait_send()
@@ -670,8 +682,8 @@
             pltpu.VMEM((HD, EDGES, 80, HEAD_DIM), BF),
             pltpu.VMEM((EDGES, 16, W), BF),
             pltpu.VMEM((EDGES, 16, W), BF),
-            pltpu.VMEM((NZ, 16, 256), BF),
-            pltpu.VMEM((NZ, 16, 256), BF),
+            pltpu.VMEM((NZ, 2, 16, HEAD_DIM), BF),
+            pltpu.VMEM((NZ, 2, 16, HEAD_DIM), BF),
             pltpu.VMEM((2, NB, 16, 256), BF),
             pltpu.VMEM((2, NB, 16, W), BF),
             dma((13,)),
@@ -682,7 +694,7 @@
             dma((3,)), dma((3,)),
             dma((HD,)), dma((HD,)), dma((HD,)), dma((HD,)),
             dma((HD, NZ)), dma((HD, NZ)),
-            dma((NZ,)), dma((NZ,)),
+            dma((2, NZ)), dma((2, NZ)),
             dma((HD, EDGES)), dma((HD, EDGES)),
             dma((EDGES,)), dma((EDGES,)),
             dma((EDGES,)), dma((EDGES,)),

time: 73.6 us -> 75.2 us (1.022)
  Pallas kernels: 71.5 us -> 73.1 us
    pallas_call x1, Pallas kernels: 69.3 us -> 70.9 us  [on_device(): pl.pallas_call(kernel, out_shape=[jax.ShapeDtypeStruct((8, ALL), BF), jax...]
where the time goes in v5:
time: 75.2 us; the launch traced here: 75 us
  Pallas kernels  73.1 us (97%)
  between operations  1.94 us (3%)
    pallas_call x1, Pallas kernels, on_device(): pl.pallas_call(kernel, out_shape=[jax.ShapeDtypeStruct((8, ALL), BF), jax...  70.9 us
    pallas_call x1, Pallas kernels, on_device(): pl.pallas_call(deliver, out_shape=shapes, in_specs=[vmem] * 3, out_specs=...  2.2 us

profile of v5, /device:TPU:1, one launch (start us, length us, event | category | flops | bytes accessed | tf_op | source)
XLA Modules:
  0.0 75.0 jit_solution(17194432339462565406)
XLA Ops:
  1.9 70.9 %joint_backward.1 = (bf16[8,3072]{1,0:T(8,128)(2,1)}, bf16[24,2,32,128]{3,2,1,0:T(8,128)(2,1)}, bf16[3,256,384]{2,1,0:T(8,128)(2,1)}) custom-call(s32[1]{0:T(128)S(6)} %copy.22.off_ref, s32[1]{0:T(128)S(6)} %copy.21.cnt_ref, bf16[8,3072]{1,0:T(8,128)(2,1)} %sq_h.1, bf16[8,3072]{1,0:T(8,128)(2,1)} %so_h.1, bf16[8,3072]{1,0:T(8,128)(2,1)} %sg_h.1, ...), custom_call_target="tpu_custom_call" | custom-call | flops 2500000000 | bytes 4000000 | tf_op jit(solution)/shard_map/joint_backward/pallas_call | solution.py:644
  72.8 2.2 %deliver.1 = (bf16[8,3072]{1,0:T(8,128)(2,1)}, bf16[32,3072]{1,0:T(8,128)(2,1)}, bf16[32,3072]{1,0:T(8,128)(2,1)}, bf16[256,384]{1,0:T(8,128)(2,1)}, bf16[256,384]{1,0:T(8,128)(2,1)}, /*index=5*/bf16[256,384]{1,0:T(8,128)(2,1)}) custom-call(bf16[8,3072]{1,0:T(8,128)(2,1)} %get-tuple-element.9.sqo, bf16[24,2,32,128]{3,2,1,0:T(8,128)(2,1)} %get-tuple-element.10.okv, ...), custom_call_target="tpu_custom_call" | custom-call | tf_op jit(solution)/shard_map/deliver/pallas_call | solution.py:719

commit v6 on v4

--- a/solution.py
+++ b/solution.py
@@ -46,6 +46,8 @@
 BELOW = {child: [k for k, e in enumerate(TREE) if e[1] == child] for child, _, _ in TREE}
 RELAYS = (1, 3, 4, 7, 6, 5)
 LEAVES = (14, 8, 9, 10, 11, 12, 13, 0, 2)
+GATHERED = ((0, 1), (1, 2))
+SUMMED = ((0, 2), (2, 1))
 AROUND = [e[2] for e in TREE[:8]]
 
 
@@ -268,9 +270,10 @@
         st[b, j : j + 1, :] = pltpu.roll(row, lax.rem(shift + HEAD_DIM - 8 * j, HEAD_DIM), 1)
     st[b, HD : 2 * HD, :] = jnp.where(here, logs, 0.0)
 
-    def ag(j, k, s, e):
-        block = qg.at[j, :, rows_of(s, ROWS), :]
-        return remote(block, block, s_xy.at[j, k], r_xy.at[j, k], on_chip(e))
+    def ag(i, k, s, e):
+        start, count = GATHERED[i]
+        block = qg.at[pl.ds(start, count), :, rows_of(s, ROWS), :]
+        return remote(block, block, s_xy.at[i, k], r_xy.at[i, k], on_chip(e))
 
     def ag_st(k, s, e):
         return remote(st.at[s], st.at[s], s_st.at[k], r_st.at[k], on_chip(e))
@@ -292,7 +295,9 @@
         for k in range(8):
             if j == 0:
                 from_parent(k, ag_st).start()
-            from_parent(k, ag_of(j)).start()
+                from_parent(k, ag_of(0)).start()
+            if j == HD - 1:
+                from_parent(k, ag_of(1)).start()
 
     def ag_relay(j):
         for k in RELAYS:
@@ -358,7 +363,6 @@
     ag_relay(0)
     text_keys(1)
     share_kv(0)
-    ag_relay(1)
     text_keys(2)
     other = rows_of(1 - c, HALF)
     sib_t = remote(dkvt.at[:, :, other, :], xt, s_sib.at[0], r_sib.at[0], sib)
@@ -405,17 +409,22 @@
         lax.fori_loop(1, NZ, go_out, 0)
         okv[h * HD + j] = dkvs[j, :, token_rows(h), :]
 
-    def make_sum(own, copy, sent, got):
+    def make_sum(own, copy, sent, got, parts):
         def gather(e, below):
-            value = own(e)
             for k in below:
                 copy(k).wait_recv()
-                value = value + got[k].astype(F32)
-            return value
+            values = []
+            for i in range(parts):
+                value = own(i, e)
+                for k in below:
+                    value = value + got(i, k)[...].astype(F32)
+                values.append(value)
+            return values
 
         def pass_on(some):
             for k in some:
-                sent[k] = gather(source(k), BELOW[TREE[k][0]]).astype(BF)
+                for i, value in enumerate(gather(source(k), BELOW[TREE[k][0]])):
+                    sent(i, k)[...] = value.astype(BF)
                 copy(k).start()
 
         return gather, pass_on
@@ -424,20 +433,23 @@
         dx, dy = TREE[k][2]
         return remote(src, dst, ss, rs, on_chip(chip(-dx, -dy)))
 
-    def rs_copy(j, k):
-        return towards_root(k, rs_s.at[j, k], rs_r.at[j, k], s_rs.at[j, k], r_rs.at[j, k])
+    def rs_copy(i, k):
+        start, count = SUMMED[i]
+        heads = pl.ds(start, count)
+        return towards_root(k, rs_s.at[heads, k], rs_r.at[heads, k], s_rs.at[i, k], r_rs.at[i, k])
 
     def tk_copy(k):
         return towards_root(k, tk_s.at[k], tk_r.at[k], s_tk.at[k], r_tk.at[k])
 
-    def own_rows(j):
-        def own(e):
+    def own_rows(start):
+        def own(i, e):
+            j = start + i
             text = dq[j, pl.ds(pl.multiple_of(SLAB_Q + e * 8, 8), 8), :]
             return jnp.concatenate([dq[j, rows_of(e, ROWS), :], text, jnp.zeros_like(text)], axis=0)
 
         return own
 
-    def own_text(e):
+    def own_text(_, e):
         at = rows_of(e, 8)
         at_half = pl.ds(pl.multiple_of(HALF * c + e * 8, 8), 8)
         heads = [
@@ -447,9 +459,18 @@
         return jnp.concatenate(heads, axis=1)
 
     rs_sums = [
-        make_sum(own_rows(j), lambda k, j=j: rs_copy(j, k), rs_s.at[j], rs_r.at[j]) for j in range(HD)
+        make_sum(
+            own_rows(start),
+            lambda k, i=i: rs_copy(i, k),
+            lambda i, k, start=start: rs_s.at[start + i, k],
+            lambda i, k, start=start: rs_r.at[start + i, k],
+            count,
+        )
+        for i, (start, count) in enumerate(SUMMED)
     ]
-    tk_gather, tk_pass = make_sum(own_text, tk_copy, tk_s, tk_r)
+    tk_gather, tk_pass = make_sum(
+        own_text, tk_copy, lambda i, k: tk_s.at[k], lambda i, k: tk_r.at[k], 1
+    )
 
     def tx_copy(k, s, e):
         return remote(tx.at[c, s], tx.at[c, s], s_tx.at[k], r_tx.at[k], on_chip(e))
@@ -477,7 +498,7 @@
     sn = sin_t[own_at, :]
 
     def text_key_result():
-        total = tk_gather(b, range(8))
+        (total,) = tk_gather(b, range(8))
         for j in range(HD):
             tkx[c, b, :, cols(j)] = jnp.concatenate(
                 [turn_back(total[:8, cols(j)], ct, sn), total[8:, cols(j)]], axis=0
@@ -490,11 +511,11 @@
     sib_t.wait()
     tk_pass(LEAVES)
     for j in range(HD):
-        if j > 0:
-            ag_rest(j)
+        if j == 1:
+            ag_rest(1)
         sib_kv(j, theirs).wait_recv()
         if j == 0:
-            ag_relay(2)
+            ag_relay(1)
         keys_t = kv[j, 0].T
         image_keys(j, keys_t, slice(SLAB_Q, SLAB_Q + HALF), True)
         for i in range(SLAB_Q // STEP):
@@ -505,23 +526,24 @@
         sib_d(j).start()
         if j < HD - 1:
             share_kv(j + 1)
-        rs_sums[j][1](LEAVES)
         if j == 0:
             tk_pass(RELAYS)
         else:
-            rs_sums[j - 1][1](RELAYS)
+            rs_sums[j - 1][1](LEAVES)
+        if j == HD - 1:
+            rs_sums[0][1](RELAYS)
         if j == 1:
             text_key_result()
         if j == 2:
             spread_on(tkx_copy)
     finish_kv(HD - 1)
-    rs_sums[HD - 1][1](RELAYS)
+    rs_sums[1][1](RELAYS)
 
     cq, sn_q = slab_angles(0, ROWS)
     parts = []
     text_parts = []
-    for j in range(HD):
-        total = rs_sums[j][0](b, range(8))
+    totals = rs_sums[0][0](b, range(8)) + rs_sums[1][0](b, range(8))
+    for j, total in enumerate(totals):
         extra = jnp.where(odd, dqt[j, ROWS + 8 : ROWS + 16, :], dqt[j, ROWS : ROWS + 8, :])
         text_parts.append(turn_back(total[ROWS : ROWS + 8, :] + extra, ct, sn))
         parts.append(turn_back(total[:ROWS, :] + dqt[j, :ROWS, :], cq, sn_q).reshape(NZ, 8, HEAD_DIM))
@@ -599,9 +621,9 @@
         from_parent(k, tx_copy).wait_send()
         from_parent(k, tkx_copy).wait_send()
         tk_copy(k).wait_send()
-        for j in range(HD):
-            from_parent(k, ag_of(j)).wait_send()
-            rs_copy(j, k).wait_send()
+        for i in range(2):
+            from_parent(k, ag_of(i)).wait_send()
+            rs_copy(i, k).wait_send()
     for j in range(HD):
         sib_kv(j, mine).wait_send()
     sib_tx.wait_send()
@@ -677,13 +699,13 @@
             dma((13,)),
             dma((2, NZ)), dma((NZ,)), dma((NZ,)),
             dma((HD, NZ)), dma((HD, NZ)),
-            dma((HD, EDGES)), dma((HD, EDGES)),
+            dma((2, EDGES)), dma((2, EDGES)),
             dma((EDGES,)), dma((EDGES,)),
             dma((3,)), dma((3,)),
             dma((HD,)), dma((HD,)), dma((HD,)), dma((HD,)),
             dma((HD, NZ)), dma((HD, NZ)),
             dma((NZ,)), dma((NZ,)),
-            dma((HD, EDGES)), dma((HD, EDGES)),
+            dma((2, EDGES)), dma((2, EDGES)),
             dma((EDGES,)), dma((EDGES,)),
             dma((EDGES,)), dma((EDGES,)),
             dma((EDGES,)), dma((EDGES,)),

time: 73.6 us -> 74.8 us (1.016)
  Pallas kernels: 71.5 us -> 72.6 us
    pallas_call x1, Pallas kernels: 69.3 us -> 70.4 us  [on_device(): pl.pallas_call(kernel, out_shape=[jax.ShapeDtypeStruct((8, ALL), BF), jax...]
where the time goes in v6:
time: 74.8 us; the launch traced here: 74.6 us
  Pallas kernels  72.6 us (97%)
  between operations  1.94 us (3%)
    pallas_call x1, Pallas kernels, on_device(): pl.pallas_call(kernel, out_shape=[jax.ShapeDtypeStruct((8, ALL), BF), jax...  70.4 us
    pallas_call x1, Pallas kernels, on_device(): pl.pallas_call(deliver, out_shape=shapes, in_specs=[vmem] * 3, out_specs=...  2.2 us

profile of v6, /device:TPU:1, one launch (start us, length us, event | category | flops | bytes accessed | tf_op | source)
XLA Modules:
  0.0 74.6 jit_solution(8739854002385506630)
XLA Ops:
  1.9 70.4 %joint_backward.1 = (bf16[8,3072]{1,0:T(8,128)(2,1)}, bf16[24,2,32,128]{3,2,1,0:T(8,128)(2,1)}, bf16[3,256,384]{2,1,0:T(8,128)(2,1)}) custom-call(s32[1]{0:T(128)S(6)} %copy.22.off_ref, s32[1]{0:T(128)S(6)} %copy.21.cnt_ref, bf16[8,3072]{1,0:T(8,128)(2,1)} %sq_h.1, bf16[8,3072]{1,0:T(8,128)(2,1)} %so_h.1, bf16[8,3072]{1,0:T(8,128)(2,1)} %sg_h.1, ...), custom_call_target="tpu_custom_call" | custom-call | flops 2500000000 | bytes 4000000 | tf_op jit(solution)/shard_map/joint_backward/pallas_call | solution.py:654
  72.4 2.2 %deliver.1 = (bf16[8,3072]{1,0:T(8,128)(2,1)}, bf16[32,3072]{1,0:T(8,128)(2,1)}, bf16[32,3072]{1,0:T(8,128)(2,1)}, bf16[256,384]{1,0:T(8,128)(2,1)}, bf16[256,384]{1,0:T(8,128)(2,1)}, /*index=5*/bf16[256,384]{1,0:T(8,128)(2,1)}) custom-call(bf16[8,3072]{1,0:T(8,128)(2,1)} %get-tuple-element.9.sqo, bf16[24,2,32,128]{3,2,1,0:T(8,128)(2,1)} %get-tuple-element.10.okv, ...), custom_call_target="tpu_custom_call" | custom-call | tf_op jit(solution)/shard_map/deliver/pallas_call | solution.py:729

commit v7 on v4

--- a/solution.py
+++ b/solution.py
@@ -356,13 +356,10 @@
 
     text_keys(0)
     ag_relay(0)
-    text_keys(1)
     share_kv(0)
     ag_relay(1)
-    text_keys(2)
     other = rows_of(1 - c, HALF)
     sib_t = remote(dkvt.at[:, :, other, :], xt, s_sib.at[0], r_sib.at[0], sib)
-    sib_t.start()
     ag_rest(0)
     for i in range(NB // 2):
         stp[:, cols(i)] = st[2 * i] + st[2 * i + 1]
@@ -487,8 +484,6 @@
     sib_tkx = remote(tkx.at[c], tkx.at[c], s_sib.at[2], r_sib.at[2], sib)
     sib_tx = remote(tx.at[c], tx.at[c], s_sib.at[1], r_sib.at[1], sib)
 
-    sib_t.wait()
-    tk_pass(LEAVES)
     for j in range(HD):
         if j > 0:
             ag_rest(j)
@@ -505,17 +500,20 @@
         sib_d(j).start()
         if j < HD - 1:
             share_kv(j + 1)
+            text_keys(j + 1)
+        if j == 1:
+            sib_t.start()
         rs_sums[j][1](LEAVES)
-        if j == 0:
-            tk_pass(RELAYS)
-        else:
+        if j > 0:
             rs_sums[j - 1][1](RELAYS)
         if j == 1:
-            text_key_result()
+            sib_t.wait()
+            tk_pass(LEAVES)
         if j == 2:
-            spread_on(tkx_copy)
+            tk_pass(RELAYS)
     finish_kv(HD - 1)
     rs_sums[HD - 1][1](RELAYS)
+    text_key_result()
 
     cq, sn_q = slab_angles(0, ROWS)
     parts = []
@@ -542,9 +540,10 @@
 
     lax.fori_loop(1, NZ, go_oq, 0)
     sqr[h] = sqs[h]
+    spread_on(tkx_copy)
+    spread_on(tx_copy)
     spread_end(tkx_copy)
     sib_tkx.start()
-    spread_on(tx_copy)
     spread_end(tx_copy)
     sib_tx.start()
 

time: 73.6 us -> 73.4 us (level)
  no operation moved by 1% of the time
where the time goes in v7:
time: 73.4 us; the launch traced here: 73 us
  Pallas kernels  71.1 us (97%)
  between operations  1.94 us (3%)
    pallas_call x1, Pallas kernels, on_device(): pl.pallas_call(kernel, out_shape=[jax.ShapeDtypeStruct((8, ALL), BF), jax...  68.9 us
    pallas_call x1, Pallas kernels, on_device(): pl.pallas_call(deliver, out_shape=shapes, in_specs=[vmem] * 3, out_specs=...  2.2 us

profile of v7, /device:TPU:1, one launch (start us, length us, event | category | flops | bytes accessed | tf_op | source)
XLA Modules:
  0.0 73.0 jit_solution(6913882710342150998)
XLA Ops:
  1.9 68.9 %joint_backward.1 = (bf16[8,3072]{1,0:T(8,128)(2,1)}, bf16[24,2,32,128]{3,2,1,0:T(8,128)(2,1)}, bf16[3,256,384]{2,1,0:T(8,128)(2,1)}) custom-call(s32[1]{0:T(128)S(6)} %copy.22.off_ref, s32[1]{0:T(128)S(6)} %copy.21.cnt_ref, bf16[8,3072]{1,0:T(8,128)(2,1)} %sq_h.1, bf16[8,3072]{1,0:T(8,128)(2,1)} %so_h.1, bf16[8,3072]{1,0:T(8,128)(2,1)} %sg_h.1, ...), custom_call_target="tpu_custom_call" | custom-call | flops 2500000000 | bytes 4000000 | tf_op jit(solution)/shard_map/joint_backward/pallas_call | solution.py:631
  70.8 2.2 %deliver.1 = (bf16[8,3072]{1,0:T(8,128)(2,1)}, bf16[32,3072]{1,0:T(8,128)(2,1)}, bf16[32,3072]{1,0:T(8,128)(2,1)}, bf16[256,384]{1,0:T(8,128)(2,1)}, bf16[256,384]{1,0:T(8,128)(2,1)}, /*index=5*/bf16[256,384]{1,0:T(8,128)(2,1)}) custom-call(bf16[8,3072]{1,0:T(8,128)(2,1)} %get-tuple-element.9.sqo, bf16[24,2,32,128]{3,2,1,0:T(8,128)(2,1)} %get-tuple-element.10.okv, ...), custom_call_target="tpu_custom_call" | custom-call | tf_op jit(solution)/shard_map/deliver/pallas_call | solution.py:706
